TPU v7x, 32 devices: a whole 2x2x4 slice. The times are simulated.
32 devices in a mesh: dp: 8 (over z, x), tensor: 4 (over y, core).
Axes of the slice: x: 2, y: 2, z: 4, core: 2. Of those that a mesh axis runs over, the one named last changes fastest.
Arguments:
- tokens: bfloat16 [8192, 2048], P('dp'), may hold values from -6 to 6
- mixer_gain: bfloat16 [2048], P('dp'), may hold values from 0.5 to 1.5
- query_weight: bfloat16 [2048, 2048], P('dp', 'tensor'), may hold values from -0.125 to 0.125
- key_weight: bfloat16 [2048, 2048], P('dp', 'tensor'), may hold values from -0.125 to 0.125
- value_weight: bfloat16 [2048, 4096], P('dp', 'tensor'), may hold values from -0.125 to 0.125
- gate_weight: bfloat16 [2048, 4096], P('dp', 'tensor'), may hold values from -0.125 to 0.125
- out_weight: bfloat16 [4096, 2048], P('tensor', 'dp'), may hold values from -0.1875 to 0.1875
- group_gain: bfloat16 [8, 512], P('tensor', 'dp'), may hold values from 0.5 to 1.5
- feed_gain: bfloat16 [2048], P('dp'), may hold values from 0.5 to 1.5
- hidden_weight: bfloat16 [2048, 4096], P('dp', 'tensor'), may hold values from -0.125 to 0.125
- up_weight: bfloat16 [2048, 4096], P('dp', 'tensor'), may hold values from -0.125 to 0.125
- down_weight: bfloat16 [4096, 2048], P('tensor', 'dp'), may hold values from -0.125 to 0.125
- cotangent: bfloat16 [8192, 2048], P('dp'), may hold values from -6 to 6
Outputs:
- output: bfloat16 [8192, 2048], P('dp')
- tokens_grad: float32 [8192, 2048], P('dp')
- mixer_gain_grad: float32 [2048], P('dp')
- query_weight_grad: float32 [2048, 2048], P('dp', 'tensor')
- key_weight_grad: float32 [2048, 2048], P('dp', 'tensor')
- value_weight_grad: float32 [2048, 4096], P('dp', 'tensor')
- gate_weight_grad: float32 [2048, 4096], P('dp', 'tensor')
- out_weight_grad: float32 [4096, 2048], P('tensor', 'dp')
- group_gain_grad: float32 [8, 512], P('tensor', 'dp')
- feed_gain_grad: float32 [2048], P('dp')
- hidden_weight_grad: float32 [2048, 4096], P('dp', 'tensor')
- up_weight_grad: float32 [2048, 4096], P('dp', 'tensor')
- down_weight_grad: float32 [4096, 2048], P('tensor', 'dp')
All inputs are finite; a program needn't handle non-finite values.
Results may differ from a plain program's by a relative error of at most 0.017.
Values may be sent and summed in bfloat16 or wider, within the bound.
A program may use at most 256 MiB of HBM per device.

v0:
```python
import jax
import jax.numpy as jnp
import numpy as np
from jax import lax
from jax.experimental import pallas as pl
from jax.experimental.pallas import tpu as pltpu
from jax.sharding import PartitionSpec as P

DK = 256
DV = 512

norm_epsilon = 1e-05
group_epsilon = 0.01
F32 = jnp.float32
BF16 = jnp.bfloat16


def layer_norm(values, scale_gain, epsilon=norm_epsilon):
    center = values - jnp.mean(values, axis=-1, keepdims=True)
    spread = jnp.mean(center * center, axis=-1, keepdims=True)
    return center * lax.rsqrt(spread + epsilon) * scale_gain


def group_norm(retained, scale_gain):
    shaped = retained.reshape(retained.shape[0], scale_gain.shape[0], scale_gain.shape[1])
    return layer_norm(shaped, scale_gain, group_epsilon).reshape(retained.shape)


def rotate(values, head_count, direction):
    length = values.shape[0]
    head_width = values.shape[1] // head_count
    half_width = head_width // 2
    places = jnp.arange(length, dtype=F32)[:, None]
    speeds = 10000.0 ** (-jnp.arange(half_width, dtype=F32) / half_width)
    angles = places * speeds[None, :]
    cosine = jnp.cos(angles)[:, None, :]
    sine_part = direction * jnp.sin(angles)[:, None, :]
    shaped = values.reshape(length, head_count, 2, half_width)
    front_half = shaped[:, :, 0]
    back_half = shaped[:, :, 1]
    turned = jnp.stack(
        [front_half * cosine - back_half * sine_part, front_half * sine_part + back_half * cosine],
        axis=2,
    )
    return turned.reshape(length, head_count * head_width)


def decays_plain(head_ids, length):
    log_rates = jnp.log1p(-jnp.exp2(-5.0 - head_ids))
    row_place = jnp.arange(length)[:, None]
    key_place = jnp.arange(length)[None, :]
    distance = jnp.maximum(row_place - key_place, 0).astype(F32)
    decays = jnp.where(
        (row_place >= key_place)[None], jnp.exp(log_rates[:, None, None] * distance[None]), 0.0
    )
    return decays


def decay_table(head_ids, length):
    decays = decays_plain(head_ids, length)
    return decays * lax.rsqrt(jnp.sum(decays, axis=-1, keepdims=True))


def plain_product(left, right):
    return jnp.dot(left, right, preferred_element_type=F32)


def row_product(left, right):
    return lax.dot_general(left, right, (((0,), (0,)), ((), ())), preferred_element_type=F32)


def back_product(left, right):
    return lax.dot_general(left, right, (((1,), (1,)), ((), ())), preferred_element_type=F32)


def core_scores(turned_query, turned_keys, decays):
    raw_scores = jnp.einsum("qhd,khd->hqk", turned_query, turned_keys, preferred_element_type=F32)
    scores = raw_scores * DK ** (-0.5) * decays
    row_totals = jnp.sum(scores, axis=-1, keepdims=True)
    denominators = jnp.sqrt(row_totals * row_totals + 1.0)
    return (scores, row_totals, denominators)


def feed_piece(hidden_pre, up_pre):
    return jax.nn.gelu(hidden_pre) * up_pre


def gate_piece(retained, gate_in, group_scale):
    return jax.nn.silu(gate_in) * group_norm(retained, group_scale)


class Ring:
    def __init__(self, name, size):
        self.name = name
        self.size = size
        self.outer = size // 2
        self.me = lax.axis_index(name)
        self.swap_pairs = [(i, i ^ 1) for i in range(size)]

    def swap(self, block):
        return lax.ppermute(block, self.name, self.swap_pairs)

    def shift(self, block, step):
        pairs = [
            (i, ((i // 2 + step) % self.outer) * 2 + i % 2) for i in range(self.size)
        ]
        return lax.ppermute(block, self.name, pairs)

    def block_at(self, place):
        turn, step = place // self.outer, place % self.outer
        outer = (self.me // 2 + self.outer - step) % self.outer
        return outer * 2 + (self.me % 2 + turn) % 2

    def place_of(self, block):
        turn = (block % 2 + self.me % 2) % 2
        step = (self.me // 2 + self.outer - block // 2) % self.outer
        return turn * self.outer + step

    def own_order(self, array, axis):
        width = array.shape[axis] // self.size
        return jnp.concatenate(
            [
                lax.dynamic_slice_in_dim(array, self.block_at(p) * width, width, axis)
                for p in range(self.size)
            ],
            axis=axis,
        )

    def true_order(self, array, axis):
        width = array.shape[axis] // self.size
        return jnp.concatenate(
            [
                lax.dynamic_slice_in_dim(array, self.place_of(b) * width, width, axis)
                for b in range(self.size)
            ],
            axis=axis,
        )

    def gather(self, block, axis):
        near = jnp.concatenate(
            [block] + [self.shift(block, s) for s in range(1, self.outer)], axis=axis
        )
        return jnp.concatenate([near, self.swap(near)], axis=axis)

    def scatter_sum(self, make_half, axis):
        far = self.swap(make_half(1).astype(BF16))
        near = make_half(0) + far.astype(F32)
        width = near.shape[axis] // self.outer
        total = lax.slice_in_dim(near, 0, width, axis=axis)
        for s in range(1, self.outer):
            part = lax.slice_in_dim(near, s * width, (s + 1) * width, axis=axis).astype(BF16)
            total = total + self.shift(part, -s).astype(F32)
        return total


def half_of(array, turn, axis):
    width = array.shape[axis] // 2
    return lax.slice_in_dim(array, turn * width, (turn + 1) * width, axis=axis)


def token_sum(ring, make_rows, rows):
    width = rows // ring.size
    outer, inner = ring.me // 2, ring.me % 2
    far = [make_rows((((outer + s) % ring.outer) * 2 + 1 - inner) * width, width) for s in range(ring.outer)]
    got = ring.swap(jnp.concatenate(far, axis=0).astype(BF16)).astype(F32)
    near = [
        make_rows((((outer + s) % ring.outer) * 2 + inner) * width, width)
        + lax.slice_in_dim(got, s * width, (s + 1) * width, axis=0)
        for s in range(ring.outer)
    ]
    total = near[0]
    for s in range(1, ring.outer):
        total = total + ring.shift(near[s].astype(BF16), s).astype(F32)
    return total


def token_gather(ring, block):
    return ring.true_order(ring.gather(block, 0), 0)


MESH = pl.DeviceIdType.MESH
ANY = pl.BlockSpec(memory_space=pl.ANY)


class Wires:
    def __init__(self, outer):
        self.outer = outer
        self.dp = lax.axis_index("dp")
        self.tensor = lax.axis_index("tensor")
        self.ring = self.dp // 2
        self.turn = self.dp % 2
        self.row = self.tensor // 2
        self.core = self.tensor % 2
        self.order = [1, outer - 1] + list(range(2, outer - 1))

    def far(self, step):
        return (lax.rem(self.ring + step, self.outer) * 2 + self.turn, self.tensor)

    def peer(self):
        return (self.ring * 2 + 1 - self.turn, self.tensor)

    def sibling(self):
        return (self.dp, self.row * 2 + 1 - self.core)

    def across(self):
        return (self.dp, (1 - self.row) * 2 + self.core)

    def block_at(self, place):
        turn, step = place // self.outer, place % self.outer
        return lax.rem(self.ring + self.outer - step, self.outer) * 2 + lax.rem(self.turn + turn, 2)

    def corner(self):
        return (self.dp, (1 - self.row) * 2 + 1 - self.core)

    def greet_all(self):
        barrier = pltpu.get_barrier_semaphore()
        partners = [(self.block_at(place), self.tensor) for place in range(1, 2 * self.outer)]
        partners += [self.sibling(), self.across(), self.corner()]
        for partner in partners:
            pl.semaphore_signal(barrier, inc=1, device_id=partner, device_id_type=MESH)
        pl.semaphore_wait(barrier, len(partners))

    def greet(self):
        barrier = pltpu.get_barrier_semaphore()
        partners = [self.far(s) for s in range(1, self.outer)]
        partners += [self.peer(), self.sibling(), self.across()]
        for partner in partners:
            pl.semaphore_signal(barrier, inc=1, device_id=partner, device_id_type=MESH)
        pl.semaphore_wait(barrier, len(partners))


def remote(src, dst, send, recv, device):
    return pltpu.make_async_remote_copy(
        src_ref=src, dst_ref=dst, send_sem=send, recv_sem=recv, device_id=device, device_id_type=MESH
    )


def tile(index, rows):
    return pl.ds(pl.multiple_of(index * rows, rows), rows)


def norm_rows(values, gain, epsilon):
    center = values - jnp.mean(values, axis=-1, keepdims=True)
    spread = jnp.mean(center * center, axis=-1, keepdims=True)
    return center * lax.rsqrt(spread + epsilon) * gain


def silu(v):
    return v * (1.0 / (1.0 + jnp.exp(-v)))


N_ITEMS = 9
GAINS, QUERY, KEY, VALUE, GATE, OUT, HIDDEN, UP, DOWN = range(N_ITEMS)
STEP = 256
PART = 128


def forward_kernel(outer, heads, dims, *refs):
    length, model, block = dims
    quarter = length // 4
    tokens, cotangent, gains, cosine, sine, row_decay, key_decay = refs[:7]
    items = (gains,) + refs[7:15]
    fulls = refs[15:24]
    (mixer_out, query_out, key_out, value_out, retained_out, gate_out, mixed_out, residual_out,
     feed_out, hidden_out, up_out, activity_out) = refs[24:36]
    (slot_a, slot_b, slot_o, wide, mixer, rq, rk, values, kept, gate_in, mixed, residual, csend, crecv, ysend,
     yrecv, cos_v, sin_v, rowd, keyd, gain_v, gain_m, gain_f, gain_g,
     loc, zs, zr, xs, xr, ts, tr, ls, os_) = refs[36:]
    wires = Wires(outer)
    rows = length // STEP
    units = slot_a.shape[1]

    def piece(item, place):
        if item in (OUT, DOWN):
            return fulls[item].at[:, pl.ds(place * block, block)]
        height = items[item].shape[0]
        return fulls[item].at[pl.ds(place * height, height)]

    last = outer - 1
    up = wires.ring < last
    down = wires.ring > 0

    def along(item, source, place, step):
        device = (jnp.clip(wires.ring + step, 0, last) * 2 + wires.turn, wires.tensor)
        return remote(source, piece(item, place), zs.at[item, place], zr.at[item, place], device)

    def climb(item, source, base):
        @pl.when(up)
        def _():
            along(item, source, base + 1, 1).start()

        @pl.when(down)
        def _():
            along(item, source, base + last, -1).start()

    def beside(item, step):
        src = items[item] if step == 0 else piece(item, step)
        return remote(src, piece(item, outer + step), xs.at[item, step], xr.at[item, step], wires.peer())

    def own(item):
        return pltpu.make_async_copy(items[item], piece(item, 0), loc.at[item])

    def issue(item, cross=True):
        own(item).start()
        climb(item, items[item], 0)
        if cross:
            beside(item, 0).start()

    def hops(item, base, cross, which=None):
        for hop in which or range(1, outer):
            @pl.when(hop <= wires.ring)
            def _():
                along(item, piece(item, base + hop), base + hop, 1).wait_recv()
                if hop < last:
                    @pl.when(up)
                    def _():
                        along(item, piece(item, base + hop), base + hop + 1, 1).start()
                if cross:
                    beside(item, hop).start()

            @pl.when(hop <= last - wires.ring)
            def _():
                place = outer - hop
                along(item, piece(item, base + place), base + place, 1).wait_recv()
                if hop < last:
                    @pl.when(down)
                    def _():
                        along(item, piece(item, base + place), base + place - 1, -1).start()
                if cross:
                    beside(item, place).start()

    def pass_on(item):
        hops(item, 0, item != DOWN)

    def climb_sent(item, base):
        @pl.when(up)
        def _():
            along(item, piece(item, base), base + 1, 1).wait_send()

        @pl.when(down)
        def _():
            along(item, piece(item, base), base + last, -1).wait_send()

        for hop in range(1, last):
            @pl.when((hop <= wires.ring) & up)
            def _():
                along(item, piece(item, base + hop), base + hop + 1, 1).wait_send()

            @pl.when((hop <= last - wires.ring) & down)
            def _():
                along(item, piece(item, base + outer - hop), base + outer - hop - 1, -1).wait_send()

    def arrived(item):
        own(item).wait()
        for step in range(outer if item != DOWN else 1):
            beside(item, step).wait_recv()

    def load(src, dst, index):
        copy = pltpu.make_async_copy(src, dst, ls.at[index])
        copy.start()
        return copy

    stores = []

    def store(src, dst):
        copy = pltpu.make_async_copy(src, dst, os_.at[len(stores)])
        copy.start()
        stores.append(copy)
        return copy

    wires.greet()
    issue(GAINS)
    issue(QUERY)
    issue(KEY)
    issue(VALUE)
    beside(DOWN, 0).start()

    def own_blocks(source, target):
        copies = []
        for place in range(2 * outer):
            at = pl.multiple_of(wires.block_at(place) * block, block)
            copies.append(load(source.at[:, pl.ds(at, block)], target.at[:, pl.ds(place * block, block)], place))
        return copies

    first = 2 * outer
    loads = own_blocks(tokens, wide)
    loads.append(load(cosine, cos_v, first))
    loads.append(load(sine, sin_v, first + 1))
    loads.append(load(row_decay, rowd, first + 2))
    loads.append(load(key_decay, keyd, first + 3))
    pass_on(GAINS)
    arrived(GAINS)
    for copy in loads:
        copy.wait()
    copy = load(fulls[GAINS], gain_v, 0)
    copy.wait()
    group = jnp.zeros((1, heads * DV), F32)
    for place in range(2 * outer):
        line = gain_v[place * 16 : place * 16 + 1, :].astype(F32)
        gain_m[:, place * block : (place + 1) * block] = line[:, :block]
        gain_f[:, place * block : (place + 1) * block] = line[:, block : 2 * block]
        group = group + line[:, 2 * block :]
    gain_g[...] = group

    @pl.loop(0, length // 128)
    def _(r):
        at = tile(r, 128)
        mixer[at, :] = norm_rows(wide[at, :].astype(F32), gain_m[...], norm_epsilon).astype(BF16)

    mine = tile(wires.tensor, quarter)
    residual[...] = wide[mine, :].astype(F32)
    mixer_store = store(mixer, mixer_out)
    pass_on(QUERY)
    pass_on(KEY)
    issue(GATE)
    pass_on(VALUE)
    issue(OUT)
    arrived(QUERY)
    arrived(KEY)
    narrow = heads * DK
    copy = load(fulls[QUERY], slot_a.at[:, pl.ds(0, narrow)], 0)
    other = load(fulls[KEY], slot_a.at[:, pl.ds(narrow, narrow)], 1)
    copy.wait()
    other.wait()

    @pl.loop(0, rows)
    def _(r):
        at = tile(r, STEP)
        both = jnp.dot(mixer[at, :], slot_a[...], preferred_element_type=F32)
        c, s = cos_v[at, :], sin_v[at, :]
        half = DK // 2
        for target, base in ((rq, 0), (rk, narrow)):
            for h in range(heads):
                lo = base + h * DK
                a, b = both[:, lo : lo + half], both[:, lo + half : lo + DK]
                target[at, h * DK : h * DK + half] = (a * c - b * s).astype(BF16)
                target[at, h * DK + half : (h + 1) * DK] = (a * s + b * c).astype(BF16)

    store(rq, query_out)
    store(rk, key_out)
    pass_on(GATE)
    issue(HIDDEN)
    arrived(VALUE)
    load(fulls[VALUE], slot_b, 0).wait()

    @pl.loop(0, rows)
    def _(r):
        at = tile(r, STEP)
        values[at, :] = jnp.dot(mixer[at, :], slot_b[...], preferred_element_type=F32).astype(BF16)

    store(values, value_out)
    for h in range(heads):
        for r in range(rows):
            at = slice(r * STEP, (r + 1) * STEP)
            upto = (r + 1) * STEP
            q = rq[at, h * DK : (h + 1) * DK]
            k = rk[:upto, h * DK : (h + 1) * DK]
            raw = lax.dot_general(q, k, (((1,), (1,)), ((), ())), preferred_element_type=F32)
            fade = rowd[at, h : h + 1] * keyd[h : h + 1, :upto]
            place = lax.broadcasted_iota(jnp.int32, (STEP, upto), 0) + r * STEP
            under = place >= lax.broadcasted_iota(jnp.int32, (STEP, upto), 1)
            scores = raw * jnp.where(under, fade, 0.0)
            total = jnp.sum(scores, axis=-1, keepdims=True)
            share = (scores * lax.rsqrt(total * total + 1.0)).astype(BF16)
            kept[at, h * DV : (h + 1) * DV] = jnp.dot(
                share, values[:upto, h * DV : (h + 1) * DV], preferred_element_type=F32
            )
    kept_store = store(kept, retained_out)
    pass_on(OUT)
    issue(UP)
    arrived(GATE)
    load(fulls[GATE], slot_a, 0).wait()

    @pl.loop(0, rows)
    def _(r):
        at = tile(r, STEP)
        gate = jnp.dot(mixer[at, :], slot_a[...], preferred_element_type=F32)
        gate_in[at, :] = gate
        for h in range(heads):
            cols = slice(h * DV, (h + 1) * DV)
            normed = norm_rows(kept[at, cols], gain_g[:, cols], group_epsilon)
            mixed[at, cols] = (silu(gate[:, cols]) * normed).astype(BF16)

    gate_store = store(gate_in, gate_out)
    mixed_store = store(mixed, mixed_out)
    pass_on(HIDDEN)
    issue(DOWN, False)
    arrived(DOWN)
    climb(DOWN, piece(DOWN, outer), outer)
    arrived(OUT)
    load(fulls[OUT], slot_o, 0).wait()

    def branch_rows(index):
        return jnp.dot(mixed[tile(index, quarter), :], slot_o[...], preferred_element_type=F32)

    def to_sibling(s):
        return remote(csend.at[s], crecv.at[s], ts.at[s], tr.at[s], wires.sibling())

    cross = remote(ysend, yrecv, ts.at[2], tr.at[2], wires.across())
    for s in (1, 0):
        owner = lax.rem(wires.row + s, 2) * 2 + 1 - wires.core
        csend[s] = branch_rows(owner).astype(BF16)
        to_sibling(s).start()
    part = branch_rows((1 - wires.row) * 2 + wires.core)
    to_sibling(1).wait_recv()
    ysend[...] = (part + crecv[1].astype(F32)).astype(BF16)
    cross.start()
    residual[...] += branch_rows(wires.tensor)
    to_sibling(0).wait_recv()
    residual[...] += crecv[0].astype(F32)
    pass_on(UP)
    hops(DOWN, 0, False, (1,))
    cross.wait_recv()
    residual[...] += yrecv[...].astype(F32)
    store(residual, residual_out)
    feed_mine = wide.at[mine]

    @pl.loop(0, quarter // 128)
    def _(r):
        at = tile(r, 128)
        ysend_rows = norm_rows(residual[at, :], gain_f[...], norm_epsilon).astype(BF16)
        feed_mine[at, :] = ysend_rows

    feed_cross = remote(feed_mine, feed_mine, ts.at[3], tr.at[3], wires.across())
    feed_near = remote(feed_mine, feed_mine, ts.at[4], tr.at[4], wires.sibling())
    theirs = wide.at[tile((1 - wires.row) * 2 + wires.core, quarter)]
    feed_far = remote(theirs, theirs, ts.at[5], tr.at[5], wires.sibling())
    feed_cross.start()
    feed_near.start()
    hops(DOWN, 0, False, (2, 3))
    hops(DOWN, outer, False, (1,))
    feed_cross.wait_recv()
    feed_far.start()
    mixer_store.wait()
    cot_loads = own_blocks(cotangent, mixer)
    hops(DOWN, outer, False, (2,))
    arrived(HIDDEN)
    load(fulls[HIDDEN], slot_b, first).wait()
    feed_near.wait_recv()
    feed_far.wait_recv()
    store(wide, feed_out)
    kept_store.wait()
    gate_store.wait()

    @pl.loop(0, rows)
    def _(r):
        at = tile(r, STEP)
        kept[at, :] = jnp.dot(wide[at, :], slot_b[...], preferred_element_type=F32)

    hops(DOWN, outer, False, (3,))
    load(fulls[DOWN], slot_o, first).wait()
    for copy in cot_loads:
        copy.wait()

    @pl.loop(0, rows)
    def _(r):
        at = tile(r, STEP)
        gate_in[at, :] = lax.dot_general(
            mixer[at, :], slot_o[...], (((1,), (1,)), ((), ())), preferred_element_type=F32
        )

    arrived(UP)
    load(fulls[UP], slot_a, first).wait()
    mixed_store.wait()

    @pl.loop(0, length // PART)
    def _(r):
        at = tile(r, PART)
        u = jnp.dot(wide[at, :], slot_a[...], preferred_element_type=F32)
        h, grads = kept[at, :], gate_in[at, :]
        t = jnp.tanh(SQRT_2_PI * (h + CUBIC * h * h * h))
        gelu = 0.5 * h * (1.0 + t)
        slope = 0.5 * (1.0 + t) + 0.5 * h * (1.0 - t * t) * (SQRT_2_PI * (1.0 + 3.0 * CUBIC * h * h))
        mixed[at, :] = (gelu * u).astype(BF16)
        slot_b[at, :] = (grads * u * slope).astype(BF16)
        slot_o[at, pl.ds(0, units)] = (grads * gelu).astype(BF16)

    store(mixed, activity_out)
    store(slot_b.at[pl.ds(0, length)], hidden_out)
    store(slot_o.at[:, pl.ds(0, units)], up_out)
    for copy in stores:
        if not any(copy is done for done in (kept_store, gate_store, mixer_store, mixed_store)):
            copy.wait()
    for s in range(2):
        to_sibling(s).wait_send()
    for copy in (cross, feed_cross, feed_near, feed_far):
        copy.wait_send()
    for item in range(N_ITEMS):
        climb_sent(item, 0)
        for step in range(outer if item != DOWN else 1):
            beside(item, step).wait_send()
    climb_sent(DOWN, outer)


def position_tables(length, heads):
    half = DK // 2
    speeds = 10000.0 ** (-np.arange(half, dtype=np.float32) / np.float32(half))
    angles = np.arange(length, dtype=np.float32)[:, None] * speeds.astype(np.float32)[None, :]
    pair = [np.cos(angles), np.sin(angles)]
    turns = [t.reshape(length // PART, PART, half).swapaxes(0, 1).reshape(PART, -1) for t in pair]
    rates = np.log1p(-np.exp2(-5.0 - np.arange(heads, dtype=np.float64)))[:, None]
    places = np.arange(length, dtype=np.float64)[None, :]
    sums = np.expm1(rates * (places + 1)) / np.expm1(rates)
    row_decay = np.exp(rates * (places - length // 2)) / np.sqrt(sums) * DK**-0.5
    key_decay = np.exp(rates * (length // 2 - places))
    return [jnp.asarray(np.asarray(t, np.float32)) for t in (*pair, np.stack(turns), row_decay, key_decay)]


def forward_fast(dp_size, tokens, cotangent, gains, tables, weights):
    outer = dp_size // 2
    length, model = tokens.shape
    block = model // dp_size
    heads = weights[0].shape[1] // DK
    units = weights[3].shape[1]
    wide = units
    shapes = [(gains.shape[0] * dp_size, gains.shape[1])]
    for place, weight in enumerate(weights):
        if place + 1 in (OUT, DOWN):
            shapes.append((weight.shape[0], model))
        else:
            shapes.append((model, weight.shape[1]))
    out_shape = [jax.ShapeDtypeStruct(s, BF16) for s in shapes]
    half = heads * DK
    for shape, kind in (
        ((length, model), BF16),
        ((length, half), BF16),
        ((length, half), BF16),
        ((length, wide), BF16),
        ((length, wide), F32),
        ((length, wide), F32),
        ((length, wide), BF16),
        ((length // 4, model), F32),
        ((length, model), BF16),
        ((length, units), BF16),
        ((length, units), BF16),
        ((length, units), BF16),
    ):
        out_shape.append(jax.ShapeDtypeStruct(shape, kind))
    quarter = length // 4
    dma = pltpu.SemaphoreType.DMA
    scratch = [
        pltpu.VMEM((model, wide), BF16),
        pltpu.VMEM((model, wide), BF16),
        pltpu.VMEM((wide, model), BF16),
        pltpu.VMEM((length, model), BF16),
        pltpu.VMEM((length, model), BF16),
        pltpu.VMEM((length, half), BF16),
        pltpu.VMEM((length, half), BF16),
        pltpu.VMEM((length, wide), BF16),
        pltpu.VMEM((length, wide), F32),
        pltpu.VMEM((length, wide), F32),
        pltpu.VMEM((length, wide), BF16),
        pltpu.VMEM((quarter, model), F32),
        pltpu.VMEM((2, quarter, model), BF16),
        pltpu.VMEM((2, quarter, model), BF16),
        pltpu.VMEM((quarter, model), BF16),
        pltpu.VMEM((quarter, model), BF16),
        pltpu.VMEM(tables[0].shape, F32),
        pltpu.VMEM(tables[1].shape, F32),
        pltpu.VMEM(tables[2].shape, F32),
        pltpu.VMEM(tables[3].shape, F32),
        pltpu.VMEM(shapes[0], BF16),
        pltpu.VMEM((1, model), F32),
        pltpu.VMEM((1, model), F32),
        pltpu.VMEM((1, heads * DV), F32),
        dma((N_ITEMS,)),
        dma((N_ITEMS, 2 * outer)),
        dma((N_ITEMS, 2 * outer)),
        dma((N_ITEMS, outer)),
        dma((N_ITEMS, outer)),
        dma((6,)),
        dma((6,)),
        dma((2 * outer + 4,)),
        dma((14,)),
    ]

    def kernel(*refs):
        forward_kernel(outer, heads, (length, model, block), *refs)

    results = pl.pallas_call(
        kernel,
        out_shape=out_shape,
        in_specs=[ANY] * (7 + len(weights)),
        out_specs=[ANY] * len(out_shape),
        scratch_shapes=scratch,
        compiler_params=pltpu.CompilerParams(
            collective_id=0, has_side_effects=True, vmem_limit_bytes=58 * 1024 * 1024
        ),
    )(tokens, cotangent, gains, *tables, *weights)
    return results[: N_ITEMS], results[N_ITEMS:]


N_GRADS = 7
(G_DOWN, G_HIDDEN, G_UP, G_OUT, G_GATE, G_VALUE, G_BOTH) = range(N_GRADS)
FLOW = (2, 3, 0, 1)
SQRT_2_PI = 0.7978845608028654
CUBIC = 0.044715


def rows_dot(left, right):
    return lax.dot_general(left, right, (((0,), (0,)), ((), ())), preferred_element_type=F32)


def back_dot(left, right):
    return lax.dot_general(left, right, (((1,), (1,)), ((), ())), preferred_element_type=F32)


def norm_back(values, grads, gain, epsilon):
    center = values - jnp.mean(values, axis=-1, keepdims=True)
    inverse = lax.rsqrt(jnp.mean(center * center, axis=-1, keepdims=True) + epsilon)
    unit = center * inverse
    u = grads * gain
    mean = jnp.mean(u, axis=-1, keepdims=True)
    slope = jnp.mean(u * unit, axis=-1, keepdims=True)
    return (u - mean - unit * slope) * inverse, grads * unit


def backward_kernel(outer, heads, dims, *refs):
    length, model, block, units = dims
    quarter = length // 4
    half = model // 2
    (tokens, cotangent, gains, query_full, key_full, value_full, gate_full, out_full, hidden_full, up_full,
     down_full, mixer_in, query_in, key_in, value_in, retained_in, gate_in, mixed_in, residual_in, feed_in,
     hidden_in, up_in, activity_in, turns, key_decay) = refs[:25]
    (output, tokens_out, near_out, z_land, vector_out, x_land, branch_land) = refs[25:32]
    (u0, u1, u2, u3, u4, act, hid, upg, both, fa, fb, x_ring, z_ring, x_stage, acc, csend, crecv, ysend, yrecv,
     stage, grad_q, value_q, keyd, gain_v, gain_m, gain_f, gain_g,
     vec_t, vec_tr, vec_d, vec_dr, vec_g,
     xs, xr, zs, zr, ts, tr, gs, gr, vs, vr, ls, fs, st, ac) = refs[32:]
    wires = Wires(outer)
    rows = length // STEP
    mine = tile(wires.tensor, quarter)
    near_rows = tile(wires.row * 2 + 1 - wires.core, quarter)
    across_index = (1 - wires.row) * 2 + wires.core
    across_rows = tile(across_index, quarter)
    corner_rows = tile((1 - wires.row) * 2 + 1 - wires.core, quarter)

    def load(src, dst, index):
        copy = pltpu.make_async_copy(src, dst, ls.at[index])
        copy.start()
        return copy

    def load_tall(src, dst, index):
        return [load(src.at[pl.ds(h * half, half)], dst.at[:, pl.ds(h * half, half)], index + h) for h in range(2)]

    def wait_all(copies):
        for copy in copies:
            copy.wait()

    def own_blocks(src, dst, index):
        copies = []
        for place in range(2 * outer):
            at = pl.multiple_of(wires.block_at(place) * block, block)
            copies.append(load(src.at[:, pl.ds(at, block)], dst.at[:, pl.ds(place * block, block)], index + place))
        return copies

    def true_blocks(src, dst, index):
        copies = []
        for place in range(2 * outer):
            at = pl.multiple_of(wires.block_at(place) * block, block)
            copies.append(load(src.at[:, pl.ds(place * block, block)], dst.at[:, pl.ds(at, block)], index + place))
        return copies

    def x_copy(item, s):
        return remote(x_ring.at[(item % 2) * outer + s], x_land.at[item, s], xs.at[item, s], xr.at[item, s], wires.peer())

    def z_copy(item, s):
        step = outer - 1 if s != outer - 1 else 1
        device = (lax.rem(wires.ring + step, outer) * 2 + wires.turn, wires.tensor)
        slot = (item % 2) * (outer - 1) + s - 1
        return remote(z_ring.at[slot], z_land.at[item, s - 1], zs.at[item, s], zr.at[item, s], device)

    def columns(place):
        return pl.ds(pl.multiple_of(place * block, block), block)

    def far(item, left, right):
        for s in FLOW:
            if item >= 2:
                x_copy(item - 2, s).wait_send()
            product = rows_dot(left[:, columns(outer + s)], right[...])
            x_ring[(item % 2) * outer + s] = product.astype(BF16)
            x_copy(item, s).start()

    def acc_copy(item):
        return pltpu.make_async_copy(acc, near_out.at[item], ac.at[item])

    def near(item, left, right):
        def staged(place, source):
            copy = pltpu.make_async_copy(source, x_stage.at[place], st.at[item, place])
            copy.start()
            return copy

        for s in FLOW:
            x_copy(item, s).wait_recv()
            copy = staged(s % 2, x_land.at[item, s])
            if s and item >= 2:
                z_copy(item - 2, s).wait_send()
            if s == 0 and item >= 1:
                acc_copy(item - 1).wait()
            product = rows_dot(left[:, columns(s)], right[...])
            copy.wait()
            product = product + x_stage[s % 2].astype(F32)
            if s == 0:
                acc[...] = product
                acc_copy(item).start()
                continue
            if s == 1:
                z_copy(item, 2).wait_recv()
                copy = staged(2, z_land.at[item, 1])
                copy.wait()
                product = product + x_stage[2].astype(F32)
            z_ring[(item % 2) * (outer - 1) + s - 1] = product.astype(BF16)
            z_copy(item, s).start()

    class Round:
        def __init__(self, index):
            self.index = index
            self.cross = remote(ysend, yrecv, ts.at[index, 2], tr.at[index, 2], wires.across())

        def to_sibling(self, s):
            return remote(csend.at[s], crecv.at[s], ts.at[self.index, s], tr.at[self.index, s], wires.sibling())

        def give(self, terms):
            for s in (1, 0):
                owner = lax.rem(wires.row + s, 2) * 2 + 1 - wires.core
                for h in range(2):
                    cols = slice(h * half, (h + 1) * half)
                    csend[s, :, cols] = terms(tile(owner, quarter), h).astype(BF16)
                self.to_sibling(s).start()

        def hand_over(self, terms):
            self.to_sibling(1).wait_recv()
            for h in range(2):
                cols = slice(h * half, (h + 1) * half)
                ysend[:, cols] = (terms(across_rows, h) + crecv[1, :, cols].astype(F32)).astype(BF16)
            self.cross.start()

        def keep(self, terms, totals, add):
            for h in range(2):
                part = terms(mine, h)
                totals[h][...] = totals[h][...] + part if add else part
            self.to_sibling(0).wait_recv()
            for h in range(2):
                totals[h][...] += crecv[0, :, h * half : (h + 1) * half].astype(F32)

        def finish(self, totals):
            self.cross.wait_recv()
            for h in range(2):
                totals[h][...] += yrecv[:, h * half : (h + 1) * half].astype(F32)
            for s in range(2):
                self.to_sibling(s).wait_send()
            self.cross.wait_send()

    class Spread:
        def __init__(self, index, source, land):
            self.cross = remote(source, land.at[mine], gs.at[index, 0], gr.at[index, 0], wires.across())
            self.near = remote(source, land.at[mine], gs.at[index, 1], gr.at[index, 1], wires.sibling())
            there = land.at[across_rows]
            self.far = remote(there, there, gs.at[index, 2], gr.at[index, 2], wires.sibling())
            self.own = pltpu.make_async_copy(source, land.at[mine], gs.at[index, 3])

        def start(self):
            self.cross.start()
            self.near.start()
            self.own.start()

        def pass_on(self):
            self.cross.wait_recv()
            self.far.start()

        def sent(self):
            self.cross.wait_send()
            self.near.wait_send()
            self.own.wait()

        def end(self):
            self.far.wait_recv()
            self.far.wait_send()

    def stream(src_a, src_b, body):
        def copies(r, slot):
            at = tile(r, PART)
            return (
                pltpu.make_async_copy(src_a.at[at], fa.at[slot, pl.ds(0, PART)], fs.at[0, slot]),
                pltpu.make_async_copy(src_b.at[at], fb.at[slot], fs.at[1, slot]),
            )

        for copy in copies(0, 0):
            copy.start()

        @pl.loop(0, length // PART)
        def _(r):
            slot = lax.rem(r, 2)

            @pl.when(r + 1 < length // PART)
            def _():
                for copy in copies(r + 1, 1 - slot):
                    copy.start()

            for copy in copies(r, slot):
                copy.wait()
            body(tile(r, PART), fa.at[slot, pl.ds(0, PART)], fb.at[slot])

    wires.greet_all()
    n = 2 * outer
    act_load = load(activity_in, act, n + 9)
    cot_loads = own_blocks(cotangent, u0, 0)
    hid_load = load(hidden_in, hid, n + 10)
    upg_load = load(up_in, upg, n + 11)
    hidden_loads = load_tall(hidden_full, u3, n + 3)
    up_loads = load_tall(up_full, u4, n + 5)
    feed_load = load(feed_in, u2, n + 2)
    down_load = load(down_full, u1, n)
    gain_load = load(gains, gain_v, n + 1)
    residual_load = load(residual_in, value_q, n + 7)
    table_load = load(key_decay, keyd, n + 8)
    act_load.wait()
    wait_all(cot_loads)
    far(G_DOWN, u0, act)
    hid_load.wait()
    upg_load.wait()
    wait_all(hidden_loads)
    wait_all(up_loads)

    def tall_terms(pairs):
        def terms(at, h):
            cols = slice(h * half, (h + 1) * half)
            total = None
            for left, right in pairs:
                part = back_dot(left[at, :], right[:, cols])
                total = part if total is None else total + part
            return total

        return terms

    feed_terms = tall_terms(((hid, u3), (upg, u4)))
    feed_round, output_round, mixer_round = Round(0), Round(1), Round(2)
    feed_round.give(feed_terms)
    feed_load.wait()
    far(G_HIDDEN, u2, hid)
    feed_round.hand_over(feed_terms)
    grad_halves = [grad_q.at[:, pl.ds(h * half, half)] for h in range(2)]
    value_halves = [value_q.at[:, pl.ds(h * half, half)] for h in range(2)]
    mixer_halves = [fa.at[h] for h in range(2)]
    feed_round.keep(feed_terms, grad_halves, False)
    table_load.wait()
    gain_load.wait()
    group = jnp.zeros((1, heads * DV), F32)
    for place in range(2 * outer):
        line = gain_v[place * 16 : place * 16 + 1, :].astype(F32)
        gain_m[:, place * block : (place + 1) * block] = line[:, :block]
        gain_f[:, place * block : (place + 1) * block] = line[:, block : 2 * block]
        group = group + line[:, 2 * block :]
    gain_g[...] = group
    vec_t[...] = jnp.zeros_like(vec_t)
    vec_d[...] = jnp.zeros_like(vec_d)
    vec_g[...] = jnp.zeros_like(vec_g)
    mixer_load = load(mixer_in, u3, n + 3)
    narrow = heads * DK
    core_loads = [load(value_in, u4.at[:, pl.ds(0, half)], n + 4),
                  load(query_in, u4.at[:, pl.ds(half, narrow)], n + 5),
                  load(key_in, u4.at[:, pl.ds(half + narrow, narrow)], n + 6)]
    residual_load.wait()
    feed_round.finish(grad_halves)

    @pl.loop(0, quarter // 128)
    def _(r):
        at = tile(r, 128)
        part, gain_part = norm_back(value_q[at, :], grad_q[at, :], gain_f[...], norm_epsilon)
        cot_at = pl.ds(pl.multiple_of(wires.tensor * quarter + r * 128, 128), 128)
        total = u0[cot_at, :].astype(F32) + part
        grad_q[at, :] = total
        stage[at, :] = total.astype(BF16)
        vec_t[1:2, :] += jnp.sum(gain_part, axis=0, keepdims=True)

    branch_spread = Spread(0, stage, branch_land)
    branch_spread.start()
    near(G_DOWN, u0, act)
    far(G_UP, u2, upg)

    down_load.wait()

    def output_terms(at, h):
        return jnp.dot(act[at, :], u1[:, h * half : (h + 1) * half], preferred_element_type=F32)

    branch_spread.near.wait_recv()
    output_round.give(output_terms)
    output_round.keep(output_terms, value_halves, True)
    branch_spread.pass_on()
    output_round.hand_over(output_terms)
    branch_spread.sent()
    out_load = load(out_full, u1, n)
    branch_loads = [load(branch_land.at[at], u0.at[at], n + 7 + i) for i, at in
                    enumerate((mine, near_rows, across_rows))]
    mixed_load = load(mixed_in, act, n + 1)
    branch_spread.far.wait_recv()
    branch_loads.append(load(branch_land.at[corner_rows], u0.at[corner_rows], n + 2))
    wait_all(branch_loads)
    out_load.wait()

    hold = both

    def gate_tile(at, r_ref, g_ref):
        grads = back_dot(u0[at, :], u1[...])
        for h in range(heads):
            cols = slice(h * DV, (h + 1) * DV)
            x, g, m = r_ref[:, cols], g_ref[:, cols], grads[:, cols]
            scale = gain_g[:, cols]
            sig = 1.0 / (1.0 + jnp.exp(-g))
            swish = g * sig
            center = x - jnp.mean(x, axis=-1, keepdims=True)
            inverse = lax.rsqrt(jnp.mean(center * center, axis=-1, keepdims=True) + group_epsilon)
            unit = center * inverse
            passed = m * swish
            hid[at, cols] = (m * unit * scale * (sig * (1.0 + g * (1.0 - sig)))).astype(BF16)
            vec_g[:, cols] += jnp.sum(passed * unit, axis=0, keepdims=True)
            u = passed * scale
            mean = jnp.mean(u, axis=-1, keepdims=True)
            slope = jnp.mean(u * unit, axis=-1, keepdims=True)
            hold[at, cols] = ((u - mean - unit * slope) * inverse).astype(BF16)

    near(G_HIDDEN, u2, hid)
    stream(retained_in, gate_in, gate_tile)
    mixed_load.wait()
    far(G_OUT, u0, act)
    mixer_load.wait()
    near(G_UP, u2, upg)
    value_loads = load_tall(value_full, u2, n + 1)
    far(G_GATE, u3, hid)
    wait_all(core_loads)

    side = DK // 2
    turn_load = load(turns, fb, n + 8)
    turn_load.wait()

    def turned_back(grads, r, count):
        a, b = grads[:, :side], grads[:, side:]
        c = jnp.concatenate([fb[0, :, (r + i) * side : (r + i + 1) * side] for i in range(count)], axis=0)
        s = jnp.concatenate([fb[1, :, (r + i) * side : (r + i + 1) * side] for i in range(count)], axis=0)
        return (a * c + b * s).astype(BF16), (b * c - a * s).astype(BF16)

    for h in range(heads):
        vcols = slice(h * DV, (h + 1) * DV)
        qcols = slice(half + h * DK, half + (h + 1) * DK)
        kcols = slice(half + narrow + h * DK, half + narrow + (h + 1) * DK)
        for r in range(length // PART):
            at = slice(r * PART, (r + 1) * PART)
            upto = (r + 1) * PART
            raw = back_dot(u4[at, qcols], u4[:upto, kcols])
            place = lax.broadcasted_iota(jnp.int32, (PART, upto), 0) + r * PART
            under = place >= lax.broadcasted_iota(jnp.int32, (PART, upto), 1)
            fade = keyd[heads + h : heads + h + 1, at].reshape(PART, 1) * keyd[h : h + 1, :upto]
            fade = jnp.where(under, fade, 0.0)
            scores = raw * fade
            total = jnp.sum(scores, axis=-1, keepdims=True)
            inverse = lax.rsqrt(total * total + 1.0)
            u1[at, :upto] = (scores * inverse).astype(BF16)
            grads = back_dot(hold[at, vcols], u4[:upto, vcols])
            inner = jnp.sum(grads * scores, axis=-1, keepdims=True)
            drop = inner * total * inverse * inverse * inverse
            raw_grad = ((grads * inverse - drop) * fade).astype(BF16)
            u1[at, half : half + upto] = raw_grad
            query_grad = jnp.dot(raw_grad, u4[:upto, kcols], preferred_element_type=F32)
            lo, hi = turned_back(query_grad, r, 1)
            upg[at, h * DK : h * DK + side] = lo
            upg[at, h * DK + side : (h + 1) * DK] = hi
        for c in range(rows):
            at = slice(c * STEP, (c + 1) * STEP)
            after = slice(c * STEP, length)
            for i in range(1, STEP // PART):
                spare = slice(c * STEP, c * STEP + i * PART)
                late = slice(c * STEP + i * PART, c * STEP + (i + 1) * PART)
                u1[spare, late] = jnp.zeros((i * PART, PART), BF16)
                u1[spare, half + c * STEP + i * PART : half + c * STEP + (i + 1) * PART] = jnp.zeros(
                    (i * PART, PART), BF16
                )
            hold_grad = rows_dot(u1[after, c * STEP : (c + 1) * STEP], hold[after, vcols])
            key_grad = rows_dot(u1[after, half + c * STEP : half + (c + 1) * STEP], u4[after, qcols])
            hold[at, vcols] = hold_grad.astype(BF16)
            lo, hi = turned_back(key_grad, c * (STEP // PART), STEP // PART)
            upg[at, narrow + h * DK : narrow + h * DK + side] = lo
            upg[at, narrow + h * DK + side : narrow + (h + 1) * DK] = hi

    gate_loads = load_tall(gate_full, u1, n + 3)
    both_loads = []
    for h in range(2):
        source = pl.ds(h * half, half)
        both_loads.append(load(query_full.at[source], u4.at[:, pl.ds(h * half, narrow)], n + 5 + 2 * h))
        both_loads.append(load(key_full.at[source], u4.at[:, pl.ds(h * half + narrow, narrow)], n + 6 + 2 * h))

    output_round.finish(value_halves)
    ysend[...] = value_q[...].astype(BF16)
    wait_all(true_blocks(ysend, stage, 0))
    output_spread = Spread(1, stage, output)
    output_spread.start()
    token_loads = []
    for place in range(2 * outer):
        at = pl.multiple_of(wires.block_at(place) * block, block)
        token_loads.append(load(tokens.at[mine, pl.ds(at, block)], ysend.at[:, pl.ds(place * block, block)], place))
    wait_all(token_loads)
    for r in range(2):
        at = slice(r * (quarter // 2), (r + 1) * (quarter // 2))
        value_q[at, :] = ysend[at, :].astype(F32)
    near(G_OUT, u0, act)
    far(G_VALUE, u3, hold)
    wait_all(gate_loads)
    wait_all(both_loads)
    wait_all(value_loads)
    mixer_terms = tall_terms(((upg, u4), (hold, u2), (hid, u1)))
    output_spread.near.wait_recv()
    mixer_round.give(mixer_terms)
    output_spread.pass_on()
    mixer_round.hand_over(mixer_terms)
    mixer_round.keep(mixer_terms, mixer_halves, False)
    near(G_GATE, u3, hid)
    far(G_BOTH, u3, upg)
    mixer_round.finish(mixer_halves)
    output_spread.sent()

    @pl.loop(0, quarter // 128)
    def _(r):
        at = tile(r, 128)
        grads = jnp.concatenate([fa[0, at, :], fa[1, at, :]], axis=1)
        part, gain_part = norm_back(value_q[at, :], grads, gain_m[...], norm_epsilon)
        ysend[at, :] = (grad_q[at, :] + part).astype(BF16)
        vec_t[0:1, :] += jnp.sum(gain_part, axis=0, keepdims=True)

    def vector_team(i, device):
        return remote(vec_t, vec_tr.at[i], vs.at[i], vr.at[i], device)

    team = (wires.sibling(), wires.across(), wires.corner())
    for i, device in enumerate(team):
        vector_team(i, device).start()
    wait_all(true_blocks(ysend, stage, 0))
    tokens_spread = Spread(2, stage, tokens_out)
    tokens_spread.start()
    for i, device in enumerate(team):
        vector_team(i, device).wait_recv()
    summed = vec_t[0:2, :]
    for i in range(3):
        summed = summed + vec_tr[i, 0:2, :]
    for place in range(2 * outer):
        vec_d[place, 0:2, :] = summed[:, place * block : (place + 1) * block]
        for i in range(heads * DV // block):
            vec_d[place, 2 + i : 3 + i, :] = vec_g[:, i * block : (i + 1) * block]

    def vector_data(place):
        device = (wires.block_at(place), wires.tensor)
        return remote(vec_d.at[place], vec_dr.at[place], vs.at[3 + place], vr.at[3 + place], device)

    for place in range(1, 2 * outer):
        vector_data(place).start()
    near(G_VALUE, u3, hold)
    tokens_spread.pass_on()
    vectors = vec_d[0]
    for place in range(1, 2 * outer):
        vector_data(place).wait_recv()
        vectors = vectors + vec_dr[place]
    vec_d[0] = vectors
    vector_store = load(vec_d.at[0], vector_out, 0)
    near(G_BOTH, u3, upg)

    vector_store.wait()
    branch_spread.far.wait_send()
    output_spread.end()
    tokens_spread.near.wait_recv()
    tokens_spread.end()
    tokens_spread.sent()
    for i, device in enumerate(team):
        vector_team(i, device).wait_send()
    for place in range(1, 2 * outer):
        vector_data(place).wait_send()
    acc_copy(N_GRADS - 1).wait()
    for item in (N_GRADS - 2, N_GRADS - 1):
        for s in range(outer):
            x_copy(item, s).wait_send()
        for s in range(1, outer):
            z_copy(item, s).wait_send()
    for item in range(N_GRADS):
        for s in (1, outer - 1):
            z_copy(item, s).wait_recv()


def backward_fast(dp_size, tokens, cotangent, fulls, kept, tables):
    outer = dp_size // 2
    length, model = tokens.shape
    block = model // dp_size
    gains, query_full, key_full, value_full, gate_full, out_full, hidden_full, up_full, down_full = fulls
    (mixer_input, turned_query, turned_keys, values, retained, gate_in, mixed, residual, feed_input, hidden_pre,
     up_pre, activity) = kept
    heads = query_full.shape[1] // DK
    units = hidden_full.shape[1]
    quarter = length // 4
    shape = jax.ShapeDtypeStruct
    out_shape = [
        shape((length, model), BF16),
        shape((length, model), BF16),
        shape((N_GRADS, block, units), F32),
        shape((N_GRADS, outer - 1, block, units), BF16),
        shape((8, block), F32),
        shape((N_GRADS, outer, block, units), BF16),
        shape((length, model), BF16),
    ]
    dma = pltpu.SemaphoreType.DMA
    vmem = pltpu.VMEM
    scratch = [vmem((length, model), BF16)] * 5 + [vmem((length, units), BF16)] * 4
    scratch += [vmem((2, STEP, units), F32), vmem((2, PART, units), F32)]
    scratch += [
        vmem((2 * outer, block, units), BF16),
        vmem((2 * (outer - 1), block, units), BF16),
        vmem((3, block, units), BF16),
        vmem((block, units), F32),
        vmem((2, quarter, model), BF16),
        vmem((2, quarter, model), BF16),
        vmem((quarter, model), BF16),
        vmem((quarter, model), BF16),
        vmem((quarter, model), BF16),
        vmem((quarter, model), F32),
        vmem((quarter, model), F32),
        vmem(tables[1].shape, F32),
        vmem(gains.shape, BF16),
        vmem((1, model), F32),
        vmem((1, model), F32),
        vmem((1, heads * DV), F32),
        vmem((8, model), F32),
        vmem((3, 8, model), F32),
        vmem((dp_size, 8, block), F32),
        vmem((dp_size, 8, block), F32),
        vmem((1, heads * DV), F32),
        dma((N_GRADS, outer)),
        dma((N_GRADS, outer)),
        dma((N_GRADS, outer)),
        dma((N_GRADS, outer)),
        dma((3, 3)),
        dma((3, 3)),
        dma((3, 4)),
        dma((3, 4)),
        dma((3 + dp_size,)),
        dma((3 + dp_size,)),
        dma((dp_size + 12,)),
        dma((2, 2)),
        dma((N_GRADS, outer)),
        dma((N_GRADS,)),
    ]

    def kernel(*refs):
        backward_kernel(outer, heads, (length, model, block, units), *refs)

    operands = (tokens, cotangent, *fulls, *kept, *tables)
    return pl.pallas_call(
        kernel,
        out_shape=out_shape,
        in_specs=[ANY] * len(operands),
        out_specs=[ANY] * len(out_shape),
        scratch_shapes=scratch,
        compiler_params=pltpu.CompilerParams(
            collective_id=1, has_side_effects=True, vmem_limit_bytes=63 * 1024 * 1024
        ),
    )(*operands)


def on_device(
    dp_size,
    tensor_size,
    tokens,
    mixer_gain,
    query_weight,
    key_weight,
    value_weight,
    gate_weight,
    out_weight,
    group_gain,
    feed_gain,
    hidden_weight,
    up_weight,
    down_weight,
    cotangent,
):
    data = Ring("dp", dp_size)
    team = Ring("tensor", tensor_size)
    length, model = tokens.shape
    quarter = length // tensor_size
    heads_here = query_weight.shape[1] // DK

    block = mixer_gain.shape[0]
    width = query_weight.shape[1]
    group_block = group_gain.shape[1]
    head_ids = (lax.axis_index("tensor") * heads_here + jnp.arange(heads_here)).astype(F32)
    decays = decay_table(head_ids, length)
    inputs = data.own_order(tokens, 1)
    cot = data.own_order(cotangent, 1)

    def my_rows(array):
        return lax.dynamic_slice_in_dim(array, team.me * quarter, quarter, 0)

    def row_terms(left, right):
        return lambda start, rows: plain_product(
            lax.dynamic_slice_in_dim(left, start, rows, 0), right
        )

    units = hidden_weight.shape[1]
    even = units == 2 * width == heads_here * DV == model // 2 and heads_here * DV // block <= 6
    if even and block % 128 == 0 and tensor_size == 4 and dp_size == 8 and length % 1024 == 0:
        group_line = lax.dynamic_update_slice(
            jnp.zeros((heads_here, DV), BF16), group_gain, (0, data.me * group_block)
        )
        gains = jnp.concatenate([mixer_gain, feed_gain, group_line.reshape(-1)])
        gains = jnp.broadcast_to(gains[None, :], (16, gains.shape[0]))
        cosine, sine, turns, row_decays, key_decays = position_tables(length, query_weight.shape[1] * tensor_size // DK)
        first = lax.axis_index("tensor") * heads_here
        row_decay = lax.dynamic_slice_in_dim(row_decays, first, heads_here, 0)
        key_decay = lax.dynamic_slice_in_dim(key_decays, first, heads_here, 0)
        tables = (cosine, sine, row_decay.T, key_decay)
        back_tables = (turns, jnp.concatenate([key_decay, row_decay]))
        fulls, kept = forward_fast(
            dp_size,
            tokens,
            cotangent,
            gains,
            tables,
            (query_weight, key_weight, value_weight, gate_weight, out_weight, hidden_weight, up_weight, down_weight),
        )
        output, tokens_grad, near_sums, landed, vectors, _, _ = backward_fast(
            dp_size, tokens, cotangent, fulls, kept, back_tables
        )
        sums = [near_sums[k] + landed[k, 0].astype(F32) + landed[k, 2].astype(F32) for k in range(N_GRADS)]
        group_scale_grad = vectors[2 : 2 + heads_here * DV // block].reshape(heads_here, DV)
        return (
            output,
            tokens_grad.astype(F32),
            vectors[0],
            sums[G_BOTH][:, :width],
            sums[G_BOTH][:, width:],
            sums[G_VALUE],
            sums[G_GATE],
            sums[G_OUT].T,
            lax.dynamic_slice_in_dim(group_scale_grad, data.me * group_block, group_block, 1),
            vectors[1],
            sums[G_HIDDEN],
            sums[G_UP],
            sums[G_DOWN].T,
        )
    else:
        gains = jnp.concatenate([mixer_gain, feed_gain, group_gain.reshape(-1)])[None, :]
        gains = data.gather(gains, 0)
        mixer_scale = gains[:, :block].reshape(-1).astype(F32)
        feed_scale = gains[:, block : 2 * block].reshape(-1).astype(F32)
        group_scale = data.true_order(gains[:, 2 * block :], 0).astype(F32)
        group_scale = group_scale.reshape(dp_size, heads_here, -1).swapaxes(0, 1).reshape(heads_here, -1)

        query_key = data.gather(jnp.concatenate([query_weight, key_weight], axis=1), 0)
        value_full = data.gather(value_weight, 0)
        gate_full = data.gather(gate_weight, 0)
        out_full = data.gather(out_weight, 1)
        hidden_full = data.gather(hidden_weight, 0)
        up_full = data.gather(up_weight, 0)
        down_full = data.gather(down_weight, 1)

        mixer_input = layer_norm(inputs.astype(F32), mixer_scale).astype(BF16)

        both = plain_product(mixer_input, query_key)
        query = both[:, :width]
        keyset = both[:, width:]
        values = plain_product(mixer_input, value_full).astype(BF16)
        gate_in = plain_product(mixer_input, gate_full)
        turned_query = rotate(query, heads_here, 1.0).astype(BF16).reshape(length, heads_here, DK)
        turned_keys = rotate(keyset, heads_here, 1.0).astype(BF16).reshape(length, heads_here, DK)
        scores, row_totals, denominators = core_scores(turned_query, turned_keys, decays)
        weights = (scores / denominators).astype(BF16)
        value_heads = values.reshape(length, heads_here, DV)
        retained = jnp.einsum("hqk,khd->qhd", weights, value_heads, preferred_element_type=F32)
        retained = retained.reshape(length, heads_here * DV)
        mixed = gate_piece(retained, gate_in, group_scale).astype(BF16)

        branch = token_sum(team, row_terms(mixed, out_full), length)
        residual = my_rows(inputs).astype(F32) + branch
        feed_input = token_gather(team, layer_norm(residual, feed_scale).astype(BF16))
        hidden_pre = plain_product(feed_input, hidden_full)
        up_pre = plain_product(feed_input, up_full)

    activity, feed_back = jax.vjp(feed_piece, hidden_pre, up_pre)
    activity = activity.astype(BF16)
    activity_grad = back_product(cot, down_full)
    hidden_grad, up_grad = feed_back(activity_grad)
    hidden_grad = hidden_grad.astype(BF16)
    up_grad = up_grad.astype(BF16)

    def feed_rows(start, rows):
        return back_product(
            lax.dynamic_slice_in_dim(hidden_grad, start, rows, 0), hidden_full
        ) + back_product(lax.dynamic_slice_in_dim(up_grad, start, rows, 0), up_full)

    feed_input_grad = token_sum(team, feed_rows, length)
    _, feed_norm_back = jax.vjp(layer_norm, residual, feed_scale)
    residual_part, feed_scale_grad = feed_norm_back(feed_input_grad)
    residual_grad = my_rows(cot).astype(F32) + residual_part
    branch_grad = token_gather(team, residual_grad.astype(BF16))

    hidden_weight_grad = data.scatter_sum(
        lambda turn: row_product(half_of(feed_input, turn, 1), hidden_grad), 0
    )
    up_weight_grad = data.scatter_sum(
        lambda turn: row_product(half_of(feed_input, turn, 1), up_grad), 0
    )
    down_grad = data.scatter_sum(lambda turn: row_product(activity, half_of(cot, turn, 1)), 1)

    feed_out = token_sum(team, row_terms(activity, down_full), length)
    output = token_gather(team, (residual + feed_out).astype(BF16))
    output = data.true_order(output, 1)

    mixed_grad = back_product(branch_grad, out_full)
    _, gate_back = jax.vjp(gate_piece, retained, gate_in, group_scale)
    retained_grad, gate_grad, group_scale_grad = gate_back(mixed_grad)
    retained_grad = retained_grad.astype(BF16)
    gate_grad = gate_grad.astype(BF16)
    out_weight_grad = data.scatter_sum(
        lambda turn: row_product(mixed, half_of(branch_grad, turn, 1)), 1
    )
    gate_weight_grad = data.scatter_sum(
        lambda turn: row_product(half_of(mixer_input, turn, 1), gate_grad), 0
    )

    grad_heads = retained_grad.reshape(length, heads_here, DV)
    weights_grad = jnp.einsum("qhd,khd->hqk", grad_heads, value_heads, preferred_element_type=F32)
    value_parts = jnp.einsum("hqk,qhd->khd", weights, grad_heads, preferred_element_type=F32)
    value_parts = value_parts.reshape(length, heads_here * DV).astype(BF16)
    value_weight_grad = data.scatter_sum(
        lambda turn: row_product(half_of(mixer_input, turn, 1), value_parts), 0
    )
    inner_totals = jnp.sum(weights_grad * scores, axis=-1, keepdims=True)
    slope = row_totals / denominators
    scores_grad = weights_grad / denominators - inner_totals / (denominators * denominators) * slope
    raw_grad = (scores_grad * DK ** (-0.5) * decays).astype(BF16)
    turned_query_grad = jnp.einsum("hqk,khd->qhd", raw_grad, turned_keys, preferred_element_type=F32)
    turned_key_grad = jnp.einsum("hqk,qhd->khd", raw_grad, turned_query, preferred_element_type=F32)
    query_parts = rotate(turned_query_grad.reshape(length, width), heads_here, -1.0).astype(BF16)
    key_parts = rotate(turned_key_grad.reshape(length, width), heads_here, -1.0).astype(BF16)
    both_parts = jnp.concatenate([query_parts, key_parts], axis=1)
    both_grad = data.scatter_sum(
        lambda turn: row_product(half_of(mixer_input, turn, 1), both_parts), 0
    )
    query_weight_grad = both_grad[:, :width]
    key_weight_grad = both_grad[:, width:]

    def mixer_rows(start, rows):
        def cut(array):
            return lax.dynamic_slice_in_dim(array, start, rows, 0)

        return (
            back_product(cut(both_parts), query_key)
            + back_product(cut(value_parts), value_full)
            + back_product(cut(gate_grad), gate_full)
        )

    mixer_input_grad = token_sum(team, mixer_rows, length)
    _, mixer_norm_back = jax.vjp(layer_norm, my_rows(inputs).astype(F32), mixer_scale)
    input_part, mixer_scale_grad = mixer_norm_back(mixer_input_grad)
    tokens_grad = token_gather(team, (residual_grad + input_part).astype(BF16))
    tokens_grad = data.true_order(tokens_grad, 1).astype(F32)

    norm_grads = jnp.concatenate([mixer_scale_grad, feed_scale_grad]).reshape(2, -1)
    norm_grads = lax.psum(data.true_order(norm_grads, 1), ("dp", "tensor"))
    norm_grads = lax.dynamic_slice_in_dim(norm_grads, data.me * block, block, 1)
    group_scale_grad = lax.psum(group_scale_grad, "dp")
    group_scale_grad = lax.dynamic_slice_in_dim(group_scale_grad, data.me * group_block, group_block, 1)
    return (
        output,
        tokens_grad,
        norm_grads[0],
        query_weight_grad,
        key_weight_grad,
        value_weight_grad,
        gate_weight_grad,
        out_weight_grad,
        group_scale_grad,
        norm_grads[1],
        hidden_weight_grad,
        up_weight_grad,
        down_grad,
    )


def solution(mesh):
    columns = P("dp", "tensor")
    rows = P("tensor", "dp")
    placed = (
        P("dp", None),
        P("dp"),
        columns,
        columns,
        columns,
        columns,
        rows,
        rows,
        P("dp"),
        columns,
        columns,
        rows,
        P("dp", None),
    )
    given = (
        P("dp", None),
        P("dp", None),
        P("dp"),
        columns,
        columns,
        columns,
        columns,
        rows,
        rows,
        P("dp"),
        columns,
        columns,
        rows,
    )

    def body(*arrays):
        return on_device(mesh.shape["dp"], mesh.shape["tensor"], *arrays)

    return jax.shard_map(body, mesh=mesh, in_specs=placed, out_specs=given, check_vma=False)
```

profile of v0, /device:TPU:0, one launch (start us, length us, event | category | flops | bytes accessed | tf_op | source)
XLA Modules:
  0.0 714.8 jit_solution(4159298533834549630)
XLA Ops:
  0.7 0.8 dynamic_update_slice.3
  1.5 0.7 pad_maximum_fusion.1
  2.1 0.8 constant_dynamic-slice_fusion.2
  2.9 0.0 copy-start.1
  2.9 0.6 pad_maximum_fusion.refs_24_
  3.6 0.6 broadcast_in_dim.10.refs_2_
  4.2 1.0 copy.31.refs_5_
  5.2 0.0 copy-done.1
  5.2 322.3 %shard_map.273 = (bf16[128,1536]{1,0:T(8,128)(2,1)}, bf16[2048,512]{1,0:T(8,128)(2,1)}, bf16[2048,512]{1,0:T(8,128)(2,1)}, bf16[2048,1024]{1,0:T(8,128)(2,1)}, b...) custom-call(bf16[1024,2048]{1,0:T(8,128)(2,1)} %refs_0_.3, ...), custom_call_target="tpu_custom_call" | custom-call | tf_op jit(solution)/shard_map/pallas_call | solution.py:680
  327.6 362.7 %shard_map.274 = (bf16[1024,2048]{1,0:T(8,128)(2,1)}, bf16[1024,2048]{1,0:T(8,128)(2,1)}, f32[7,256,1024]{2,1,0:T(8,128)}, bf16[7,3,256,1024]{3,2,1,0:T(8,128)(2...) custom-call(bf16[1024,2048]{1,0:T(8,128)(2,1)} %refs_0_.3, ...), custom_call_target="tpu_custom_call" | custom-call | tf_op jit(solution)/shard_map/pallas_call | solution.py:1250
  690.2 1.3 fusion.3
  691.6 0.7 slice.93
  692.3 0.6 constant_dynamic-slice_fusion
  692.9 1.7 convert_add_fusion.12
  694.7 7.2 %fusion = (f32[1024,256]{0,1:T(8,128)S(1)}, f32[256,1024]{1,0:T(8,128)}, f32[256,1024]{1,0:T(8,128)}, f32[1024,256]{0,1:T(8,128)S(1)}, f32[256,1024]{1,0:T(8,128)}, /*index=5*/f32[256,1024]{1,0:T(8,128)}) fusion(f32[7,256,1024]{2,1,0:T(8,128)} %get-tuple-element.63, bf16[7,3,256,1024]{3,2,1,0:T(8,128)(2,1)} %get-tuple-element.64), kind=kLoop, calls=%fused_computation.1 | loop fusion | flops 6291456 | bytes 18874368 | tf_op jit(solution)/shard_map/transpose | solution.py:1341
  701.9 1.3 copy.33
  703.2 1.0 fusion.2
  704.3 1.3 copy.32
  705.6 0.0 copy-start
  705.6 6.8 convert_element_type.87
  712.4 0.0 copy-done
  712.4 2.0 copy.37
  (3 shorter events, 0.0 us)
Async XLA Ops:
  2.9 2.3 copy-start.1
  705.6 6.8 copy-start
where the time goes:
time: 722 us; the launch traced here: 715 us
  Pallas kernels  685 us (95%)
  other arithmetic  17.1 us (2%)
  local copies, waits for them, and re-layouts  11.6 us (2%)
    pallas_call x1, Pallas kernels, backward_fast(): pl.pallas_call(kernel, out_shape=out_shape, in_specs=[ANY] * len(operands...  363 us
    pallas_call x1, Pallas kernels, forward_fast(): pl.pallas_call(kernel, out_shape=out_shape, in_specs=[ANY] * (7 + len(wei...  322 us

commit v1 on v0

--- a/solution.py
+++ b/solution.py
@@ -220,14 +220,6 @@
             pl.semaphore_signal(barrier, inc=1, device_id=partner, device_id_type=MESH)
         pl.semaphore_wait(barrier, len(partners))
 
-    def greet(self):
-        barrier = pltpu.get_barrier_semaphore()
-        partners = [self.far(s) for s in range(1, self.outer)]
-        partners += [self.peer(), self.sibling(), self.across()]
-        for partner in partners:
-            pl.semaphore_signal(barrier, inc=1, device_id=partner, device_id_type=MESH)
-        pl.semaphore_wait(barrier, len(partners))
-
 
 def remote(src, dst, send, recv, device):
     return pltpu.make_async_remote_copy(
@@ -301,7 +293,6 @@
         return pltpu.make_async_copy(items[item], piece(item, 0), loc.at[item])
 
     def issue(item, cross=True):
-        own(item).start()
         climb(item, items[item], 0)
         if cross:
             beside(item, 0).start()
@@ -368,8 +359,17 @@
         stores.append(copy)
         return copy
 
-    wires.greet()
-    issue(GAINS)
+    def gain_copy(place):
+        turn, step = place // outer, place % outer
+        there = piece(GAINS, turn * outer + (outer - step) % outer)
+        device = (wires.block_at(place), wires.tensor)
+        return remote(gains, there, zs.at[GAINS, place], zr.at[GAINS, turn * outer + (outer - step) % outer], device)
+
+    wires.greet_all()
+    for place in range(1, 2 * outer):
+        gain_copy(place).start()
+    for item in range(N_ITEMS):
+        own(item).start()
     issue(QUERY)
     issue(KEY)
     issue(VALUE)
@@ -388,8 +388,9 @@
     loads.append(load(sine, sin_v, first + 1))
     loads.append(load(row_decay, rowd, first + 2))
     loads.append(load(key_decay, keyd, first + 3))
-    pass_on(GAINS)
-    arrived(GAINS)
+    own(GAINS).wait()
+    for place in range(1, 2 * outer):
+        gain_copy(place).wait_recv()
     for copy in loads:
         copy.wait()
     copy = load(fulls[GAINS], gain_v, 0)
@@ -585,7 +586,9 @@
         to_sibling(s).wait_send()
     for copy in (cross, feed_cross, feed_near, feed_far):
         copy.wait_send()
-    for item in range(N_ITEMS):
+    for place in range(1, 2 * outer):
+        gain_copy(place).wait_send()
+    for item in range(1, N_ITEMS):
         climb_sent(item, 0)
         for step in range(outer if item != DOWN else 1):
             beside(item, step).wait_send()
@@ -692,7 +695,7 @@
 
 N_GRADS = 7
 (G_DOWN, G_HIDDEN, G_UP, G_OUT, G_GATE, G_VALUE, G_BOTH) = range(N_GRADS)
-FLOW = (2, 3, 0, 1)
+FLOW = (2, 3, 1, 0)
 SQRT_2_PI = 0.7978845608028654
 CUBIC = 0.044715
 
@@ -723,7 +726,7 @@
      down_full, mixer_in, query_in, key_in, value_in, retained_in, gate_in, mixed_in, residual_in, feed_in,
      hidden_in, up_in, activity_in, turns, key_decay) = refs[:25]
     (output, tokens_out, near_out, z_land, vector_out, x_land, branch_land) = refs[25:32]
-    (u0, u1, u2, u3, u4, act, hid, upg, both, fa, fb, x_ring, z_ring, x_stage, acc, csend, crecv, ysend, yrecv,
+    (u0, u1, u2, u3, u4, act, hid, upg, both, fa, fb, x_ring, x_extra, z_ring, x_stage, acc, csend, crecv, ysend, yrecv,
      stage, grad_q, value_q, keyd, gain_v, gain_m, gain_f, gain_g,
      vec_t, vec_tr, vec_d, vec_dr, vec_g,
      xs, xr, zs, zr, ts, tr, gs, gr, vs, vr, ls, fs, st, ac) = refs[32:]
@@ -762,7 +765,8 @@
         return copies
 
     def x_copy(item, s):
-        return remote(x_ring.at[(item % 2) * outer + s], x_land.at[item, s], xs.at[item, s], xr.at[item, s], wires.peer())
+        source = x_extra if item == G_DOWN else x_ring.at[(item % 2) * outer + s]
+        return remote(source, x_land.at[item, s], xs.at[item, s], xr.at[item, s], wires.peer())
 
     def z_copy(item, s):
         step = outer - 1 if s != outer - 1 else 1
@@ -773,29 +777,70 @@
     def columns(place):
         return pl.ds(pl.multiple_of(place * block, block), block)
 
-    def far(item, left, right):
-        for s in FLOW:
-            if item >= 2:
+    def far(item, left, right, flow=FLOW, behind=None):
+        for s in flow:
+            if item >= 3:
                 x_copy(item - 2, s).wait_send()
             product = rows_dot(left[:, columns(outer + s)], right[...])
             x_ring[(item % 2) * outer + s] = product.astype(BF16)
-            x_copy(item, s).start()
+            if behind is None:
+                x_copy(item, s).start()
+        if behind is not None:
+            behind.wait_send()
+            for s in flow:
+                x_copy(item, s).start()
 
     def acc_copy(item):
         return pltpu.make_async_copy(acc, near_out.at[item], ac.at[item])
 
-    def near(item, left, right):
-        def staged(place, source):
-            copy = pltpu.make_async_copy(source, x_stage.at[place], st.at[item, place])
-            copy.start()
-            return copy
-
-        for s in FLOW:
+    def staged(item, place, source):
+        copy = pltpu.make_async_copy(source, x_stage.at[place], st.at[item, place])
+        copy.start()
+        return copy
+
+    sides = ((0, G_DOWN), (1, N_GRADS))
+
+    def down_product(turn, s):
+        return rows_dot(u0[:, columns(turn * outer + s)], act[...])
+
+    def down_give(s):
+        for turn, item in sides:
+            z_ring[(item % 2) * (outer - 1) + s - 1] = down_product(turn, s).astype(BF16)
+            z_copy(item, s).start()
+
+    def down_first():
+        down_give(2)
+        for turn, item in sides:
+            z_ring[(item % 2) * (outer - 1)] = down_product(turn, 1).astype(BF16)
+        x_extra[...] = down_product(1, 0).astype(BF16)
+        acc[...] = down_product(0, 0)
+        acc_copy(G_DOWN).start()
+
+    def relay(item):
+        z_copy(item, 2).wait_recv()
+        staged(item, 2, z_land.at[item, 1]).wait()
+        slot = (item % 2) * (outer - 1)
+        z_ring[slot] = (z_ring[slot].astype(F32) + x_stage[2].astype(F32)).astype(BF16)
+        z_copy(item, 1).start()
+
+    def down_sum():
+        z_copy(N_GRADS, 3).wait_recv()
+        copy = staged(N_GRADS, 2, z_land.at[N_GRADS, 2])
+        z_copy(N_GRADS, 1).wait_recv()
+        other = staged(N_GRADS, 3, z_land.at[N_GRADS, 0])
+        copy.wait()
+        other.wait()
+        total = x_extra[...].astype(F32) + x_stage[2].astype(F32) + x_stage[3].astype(F32)
+        x_extra[...] = total.astype(BF16)
+
+    def near(item, left, right, flow=FLOW):
+        before = N_GRADS if item == 1 else item - 2
+        for s in flow:
             x_copy(item, s).wait_recv()
-            copy = staged(s % 2, x_land.at[item, s])
-            if s and item >= 2:
-                z_copy(item - 2, s).wait_send()
-            if s == 0 and item >= 1:
+            copy = staged(item, s % 2, x_land.at[item, s])
+            if s:
+                z_copy(before, s).wait_send()
+            if s == 0:
                 acc_copy(item - 1).wait()
             product = rows_dot(left[:, columns(s)], right[...])
             copy.wait()
@@ -804,13 +849,9 @@
                 acc[...] = product
                 acc_copy(item).start()
                 continue
-            if s == 1:
-                z_copy(item, 2).wait_recv()
-                copy = staged(2, z_land.at[item, 1])
-                copy.wait()
-                product = product + x_stage[2].astype(F32)
             z_ring[(item % 2) * (outer - 1) + s - 1] = product.astype(BF16)
-            z_copy(item, s).start()
+            if s > 1:
+                z_copy(item, s).start()
 
     class Round:
         def __init__(self, index):
@@ -903,21 +944,23 @@
 
     wires.greet_all()
     n = 2 * outer
+    hid_load = load(hidden_in, hid, n + 10)
+    feed_load = load(feed_in, u2, n + 2)
     act_load = load(activity_in, act, n + 9)
     cot_loads = own_blocks(cotangent, u0, 0)
-    hid_load = load(hidden_in, hid, n + 10)
     upg_load = load(up_in, upg, n + 11)
     hidden_loads = load_tall(hidden_full, u3, n + 3)
     up_loads = load_tall(up_full, u4, n + 5)
-    feed_load = load(feed_in, u2, n + 2)
     down_load = load(down_full, u1, n)
     gain_load = load(gains, gain_v, n + 1)
     residual_load = load(residual_in, value_q, n + 7)
     table_load = load(key_decay, keyd, n + 8)
+    hid_load.wait()
+    feed_load.wait()
+    far(G_HIDDEN, u2, hid)
     act_load.wait()
     wait_all(cot_loads)
-    far(G_DOWN, u0, act)
-    hid_load.wait()
+    down_first()
     upg_load.wait()
     wait_all(hidden_loads)
     wait_all(up_loads)
@@ -936,8 +979,7 @@
     feed_terms = tall_terms(((hid, u3), (upg, u4)))
     feed_round, output_round, mixer_round = Round(0), Round(1), Round(2)
     feed_round.give(feed_terms)
-    feed_load.wait()
-    far(G_HIDDEN, u2, hid)
+    far(G_UP, u2, upg)
     feed_round.hand_over(feed_terms)
     grad_halves = [grad_q.at[:, pl.ds(h * half, half)] for h in range(2)]
     value_halves = [value_q.at[:, pl.ds(h * half, half)] for h in range(2)]
@@ -960,6 +1002,7 @@
     core_loads = [load(value_in, u4.at[:, pl.ds(0, half)], n + 4),
                   load(query_in, u4.at[:, pl.ds(half, narrow)], n + 5),
                   load(key_in, u4.at[:, pl.ds(half + narrow, narrow)], n + 6)]
+    down_give(3)
     residual_load.wait()
     feed_round.finish(grad_halves)
 
@@ -975,8 +1018,9 @@
 
     branch_spread = Spread(0, stage, branch_land)
     branch_spread.start()
-    near(G_DOWN, u0, act)
-    far(G_UP, u2, upg)
+    relay(G_DOWN)
+    relay(N_GRADS)
+    near(G_HIDDEN, u2, hid, (2, 3, 0))
 
     down_load.wait()
 
@@ -1019,10 +1063,11 @@
             slope = jnp.mean(u * unit, axis=-1, keepdims=True)
             hold[at, cols] = ((u - mean - unit * slope) * inverse).astype(BF16)
 
-    near(G_HIDDEN, u2, hid)
-    stream(retained_in, gate_in, gate_tile)
     mixed_load.wait()
     far(G_OUT, u0, act)
+    near(G_HIDDEN, u2, hid, (1,))
+    stream(retained_in, gate_in, gate_tile)
+    relay(G_HIDDEN)
     mixer_load.wait()
     near(G_UP, u2, upg)
     value_loads = load_tall(value_full, u2, n + 1)
@@ -1088,6 +1133,9 @@
         both_loads.append(load(query_full.at[source], u4.at[:, pl.ds(h * half, narrow)], n + 5 + 2 * h))
         both_loads.append(load(key_full.at[source], u4.at[:, pl.ds(h * half + narrow, narrow)], n + 6 + 2 * h))
 
+    down_sum()
+    relay(G_UP)
+
     output_round.finish(value_halves)
     ysend[...] = value_q[...].astype(BF16)
     wait_all(true_blocks(ysend, stage, 0))
@@ -1112,8 +1160,7 @@
     output_spread.pass_on()
     mixer_round.hand_over(mixer_terms)
     mixer_round.keep(mixer_terms, mixer_halves, False)
-    near(G_GATE, u3, hid)
-    far(G_BOTH, u3, upg)
+    relay(G_OUT)
     mixer_round.finish(mixer_halves)
     output_spread.sent()
 
@@ -1134,6 +1181,8 @@
     wait_all(true_blocks(ysend, stage, 0))
     tokens_spread = Spread(2, stage, tokens_out)
     tokens_spread.start()
+    near(G_GATE, u3, hid)
+    far(G_BOTH, u3, upg, (2, 3))
     for i, device in enumerate(team):
         vector_team(i, device).wait_recv()
     summed = vec_t[0:2, :]
@@ -1150,15 +1199,22 @@
 
     for place in range(1, 2 * outer):
         vector_data(place).start()
+    tokens_spread.pass_on()
+    relay(G_GATE)
     near(G_VALUE, u3, hold)
-    tokens_spread.pass_on()
+    relay(G_VALUE)
+    far(G_BOTH, u3, upg, (1, 0), x_copy(G_BOTH, 2))
+    x_copy(G_DOWN, 0).start()
+    near(G_BOTH, u3, upg, (2, 3))
+    near(G_BOTH, u3, upg, (1,))
+    relay(G_BOTH)
+    near(G_BOTH, u3, upg, (0,))
     vectors = vec_d[0]
     for place in range(1, 2 * outer):
         vector_data(place).wait_recv()
         vectors = vectors + vec_dr[place]
     vec_d[0] = vectors
     vector_store = load(vec_d.at[0], vector_out, 0)
-    near(G_BOTH, u3, upg)
 
     vector_store.wait()
     branch_spread.far.wait_send()
@@ -1171,9 +1227,11 @@
     for place in range(1, 2 * outer):
         vector_data(place).wait_send()
     acc_copy(N_GRADS - 1).wait()
+    x_copy(G_DOWN, 0).wait()
     for item in (N_GRADS - 2, N_GRADS - 1):
         for s in range(outer):
-            x_copy(item, s).wait_send()
+            if (item, s) != (G_BOTH, 2):
+                x_copy(item, s).wait_send()
         for s in range(1, outer):
             z_copy(item, s).wait_send()
     for item in range(N_GRADS):
@@ -1196,7 +1254,7 @@
         shape((length, model), BF16),
         shape((length, model), BF16),
         shape((N_GRADS, block, units), F32),
-        shape((N_GRADS, outer - 1, block, units), BF16),
+        shape((N_GRADS + 1, outer - 1, block, units), BF16),
         shape((8, block), F32),
         shape((N_GRADS, outer, block, units), BF16),
         shape((length, model), BF16),
@@ -1207,8 +1265,9 @@
     scratch += [vmem((2, STEP, units), F32), vmem((2, PART, units), F32)]
     scratch += [
         vmem((2 * outer, block, units), BF16),
+        vmem((block, units), BF16),
         vmem((2 * (outer - 1), block, units), BF16),
-        vmem((3, block, units), BF16),
+        vmem((4, block, units), BF16),
         vmem((block, units), F32),
         vmem((2, quarter, model), BF16),
         vmem((2, quarter, model), BF16),
@@ -1229,8 +1288,8 @@
         vmem((1, heads * DV), F32),
         dma((N_GRADS, outer)),
         dma((N_GRADS, outer)),
-        dma((N_GRADS, outer)),
-        dma((N_GRADS, outer)),
+        dma((N_GRADS + 1, outer)),
+        dma((N_GRADS + 1, outer)),
         dma((3, 3)),
         dma((3, 3)),
         dma((3, 4)),
@@ -1239,7 +1298,7 @@
         dma((3 + dp_size,)),
         dma((dp_size + 12,)),
         dma((2, 2)),
-        dma((N_GRADS, outer)),
+        dma((N_GRADS + 1, outer)),
         dma((N_GRADS,)),
     ]
 
@@ -1256,6 +1315,71 @@
         compiler_params=pltpu.CompilerParams(
             collective_id=1, has_side_effects=True, vmem_limit_bytes=63 * 1024 * 1024
         ),
+    )(*operands)
+
+
+def finish(near_sums, z_land, x_land, tokens_grad, output):
+    steps = 8
+    _, block, units = near_sums.shape
+    length, model = output.shape
+    rows, across = block // steps, block // 128
+    side = units * across // steps
+    turned = (G_DOWN, G_OUT)
+    order = (G_BOTH, G_VALUE, G_GATE, G_OUT, G_HIDDEN, G_UP, G_DOWN)
+    operands, in_specs, out_specs, out_shape = [], [], [], []
+
+    def add(array, lead, item):
+        operands.append(array)
+        if item in turned:
+            in_specs.append(pl.BlockSpec((1,) * len(lead) + (128, side), lambda i: (*lead, i % across, i // across)))
+        else:
+            in_specs.append(pl.BlockSpec((1,) * len(lead) + (rows, units), lambda i: (*lead, i, 0)))
+
+    for item in order:
+        add(near_sums, (item,), item)
+        add(z_land, (item, 0), item)
+        add(z_land, (item, 2), item)
+        if item == G_DOWN:
+            add(x_land, (item, 0), item)
+        if item == G_BOTH:
+            shapes = [((block, units // 2), (rows, units // 2))] * 2
+        else:
+            shapes = [((block, units), (rows, units))]
+        for whole, part in shapes:
+            if item in turned:
+                out_shape.append(jax.ShapeDtypeStruct((units, block), F32))
+                out_specs.append(pl.BlockSpec((side, 128), lambda i: (i // across, i % across)))
+            else:
+                out_shape.append(jax.ShapeDtypeStruct(whole, F32))
+                out_specs.append(pl.BlockSpec(part, lambda i: (i, 0)))
+    for array, kind in ((tokens_grad, F32), (output, BF16)):
+        operands.append(array)
+        spec = pl.BlockSpec((length // steps, model), lambda i: (i, 0))
+        in_specs.append(spec)
+        out_specs.append(spec)
+        out_shape.append(jax.ShapeDtypeStruct(array.shape, kind))
+
+    def kernel(*refs):
+        ins, outs = list(refs[: len(operands)]), list(refs[len(operands) :])
+        for item in order:
+            total = ins.pop(0)[0]
+            for _ in range(3 if item == G_DOWN else 2):
+                total = total + ins.pop(0)[0, 0].astype(F32)
+            if item == G_BOTH:
+                outs.pop(0)[...] = total[:, : units // 2]
+                outs.pop(0)[...] = total[:, units // 2 :]
+            else:
+                outs.pop(0)[...] = total.T if item in turned else total
+        for source, target in zip(ins, outs):
+            target[...] = source[...].astype(target.dtype)
+
+    return pl.pallas_call(
+        kernel,
+        grid=(steps,),
+        out_shape=out_shape,
+        in_specs=in_specs,
+        out_specs=out_specs,
+        compiler_params=pltpu.CompilerParams(vmem_limit_bytes=62 * 1024 * 1024),
     )(*operands)
 
 
@@ -1320,25 +1444,26 @@
             tables,
             (query_weight, key_weight, value_weight, gate_weight, out_weight, hidden_weight, up_weight, down_weight),
         )
-        output, tokens_grad, near_sums, landed, vectors, _, _ = backward_fast(
+        output, tokens_grad, near_sums, landed, vectors, crossed, _ = backward_fast(
             dp_size, tokens, cotangent, fulls, kept, back_tables
         )
-        sums = [near_sums[k] + landed[k, 0].astype(F32) + landed[k, 2].astype(F32) for k in range(N_GRADS)]
+        (query_grad, key_grad, value_grad, gate_grad, out_grad, hidden_grad, up_grad, down_grad, tokens_grad,
+         output) = finish(near_sums, landed, crossed, tokens_grad, output)
         group_scale_grad = vectors[2 : 2 + heads_here * DV // block].reshape(heads_here, DV)
         return (
             output,
-            tokens_grad.astype(F32),
+            tokens_grad,
             vectors[0],
-            sums[G_BOTH][:, :width],
-            sums[G_BOTH][:, width:],
-            sums[G_VALUE],
-            sums[G_GATE],
-            sums[G_OUT].T,
+            query_grad,
+            key_grad,
+            value_grad,
+            gate_grad,
+            out_grad,
             lax.dynamic_slice_in_dim(group_scale_grad, data.me * group_block, group_block, 1),
             vectors[1],
-            sums[G_HIDDEN],
-            sums[G_UP],
-            sums[G_DOWN].T,
+            hidden_grad,
+            up_grad,
+            down_grad,
         )
     else:
         gains = jnp.concatenate([mixer_gain, feed_gain, group_gain.reshape(-1)])[None, :]

time: 722 us -> 640 us (0.89)
  Pallas kernels: 685 us -> 626 us
  other arithmetic: 17.1 us -> 1.3 us
    pallas_call x1, Pallas kernels: 363 us -> 293 us  [backward_fast(): pl.pallas_call(kernel, out_shape=out_shape, in_specs=[ANY] * len(operands...]
    pallas_call x0 -> x1, Pallas kernels: none -> 15.6 us  [finish(): pl.pallas_call(kernel, grid=(steps,), out_shape=out_shape, in_specs=in_sp...]
    transpose x1 -> x0, other arithmetic: 7.24 us -> none  [on_device(): sums[G_DOWN]]
where the time goes in v1:
time: 640 us; the launch traced here: 633 us
  Pallas kernels  626 us (98%)
    pallas_call x1, Pallas kernels, forward_fast(): pl.pallas_call(kernel, out_shape=out_shape, in_specs=[ANY] * (7 + len(wei...  317 us
    pallas_call x1, Pallas kernels, backward_fast(): pl.pallas_call(kernel, out_shape=out_shape, in_specs=[ANY] * len(operands...  293 us
    pallas_call x1, Pallas kernels, finish(): pl.pallas_call(kernel, grid=(steps,), out_shape=out_shape, in_specs=in_sp...  15.6 us

profile of v1, /device:TPU:0, one launch (start us, length us, event | category | flops | bytes accessed | tf_op | source)
XLA Modules:
  0.0 632.9 jit_solution(1650122105239707021)
XLA Ops:
  0.7 0.8 dynamic_update_slice.3
  1.5 0.7 pad_maximum_fusion.1
  2.1 0.8 constant_dynamic-slice_fusion.2
  2.9 0.0 copy-start
  2.9 0.6 pad_maximum_fusion.refs_24_
  3.6 0.6 broadcast_in_dim.10.refs_2_
  4.2 1.0 copy.31.refs_5_
  5.2 0.0 copy-done
  5.2 317.1 %shard_map.273 = (bf16[128,1536]{1,0:T(8,128)(2,1)}, bf16[2048,512]{1,0:T(8,128)(2,1)}, bf16[2048,512]{1,0:T(8,128)(2,1)}, bf16[2048,1024]{1,0:T(8,128)(2,1)}, b...) custom-call(bf16[1024,2048]{1,0:T(8,128)(2,1)} %refs_0_.3, ...), custom_call_target="tpu_custom_call" | custom-call | tf_op jit(solution)/shard_map/pallas_call | solution.py:683
  322.3 293.3 %shard_map.274 = (bf16[1024,2048]{1,0:T(8,128)(2,1)}, bf16[1024,2048]{1,0:T(8,128)(2,1)}, f32[7,256,1024]{2,1,0:T(8,128)}, bf16[8,3,256,1024]{3,2,1,0:T(8,128)(2...) custom-call(bf16[1024,2048]{1,0:T(8,128)(2,1)} %refs_0_.3, ...), custom_call_target="tpu_custom_call" | custom-call | tf_op jit(solution)/shard_map/pallas_call | solution.py:1309
  615.6 0.0 copy-start.1
  615.6 15.6 %shard_map.275 = (f32[256,512]{1,0:T(8,128)}, f32[256,512]{1,0:T(8,128)}, f32[256,1024]{1,0:T(8,128)}, f32[256,1024]{1,0:T(8,128)}, f32[1024,256]{1,0:T(8,128)},...) custom-call(f32[7,256,1024]{2,1,0:T(8,128)} %get-tuple-element.71.re, ...), custom_call_target="tpu_custom_call" | custom-call | tf_op jit(solution)/shard_map/pallas_call | solution.py:1376
  631.3 0.0 copy-done.1
  631.3 0.6 fusion
  631.9 0.6 constant_dynamic-slice_fusion
  (4 shorter events, 0.0 us)
Async XLA Ops:
  2.9 2.3 copy-start
  615.6 15.6 %copy-start.1 = (f32[8,256]{1,0:T(8,128)S(1)}, f32[8,256]{1,0:T(8,128)}, u32[]{:S(2)}) copy-start(f32[8,256]{1,0:T(8,128)} %get-tuple-element.78) | copy-start | bytes 24580

commit v2 on v1

--- a/solution.py
+++ b/solution.py
@@ -342,7 +342,8 @@
                 along(item, piece(item, base + outer - hop), base + outer - hop - 1, -1).wait_send()
 
     def arrived(item):
-        own(item).wait()
+        if item != UP:
+            own(item).wait()
         for step in range(outer if item != DOWN else 1):
             beside(item, step).wait_recv()
 
@@ -416,6 +417,7 @@
     issue(GATE)
     pass_on(VALUE)
     issue(OUT)
+    hops(GATE, 0, True, (1,))
     arrived(QUERY)
     arrived(KEY)
     narrow = heads * DK
@@ -439,8 +441,9 @@
 
     store(rq, query_out)
     store(rk, key_out)
-    pass_on(GATE)
+    hops(GATE, 0, True, (2, 3))
     issue(HIDDEN)
+    hops(OUT, 0, True, (1,))
     arrived(VALUE)
     load(fulls[VALUE], slot_b, 0).wait()
 
@@ -467,8 +470,9 @@
                 share, values[:upto, h * DV : (h + 1) * DV], preferred_element_type=F32
             )
     kept_store = store(kept, retained_out)
-    pass_on(OUT)
+    hops(OUT, 0, True, (2, 3))
     issue(UP)
+    hops(HIDDEN, 0, True, (1,))
     arrived(GATE)
     load(fulls[GATE], slot_a, 0).wait()
 
@@ -482,14 +486,17 @@
             normed = norm_rows(kept[at, cols], gain_g[:, cols], group_epsilon)
             mixed[at, cols] = (silu(gate[:, cols]) * normed).astype(BF16)
 
+    mixer_store.wait()
+    cot_loads = own_blocks(cotangent, mixer)
     gate_store = store(gate_in, gate_out)
     mixed_store = store(mixed, mixed_out)
-    pass_on(HIDDEN)
+    hops(HIDDEN, 0, True, (2, 3))
+    hops(UP, 0, True, (1,))
     issue(DOWN, False)
     arrived(DOWN)
     climb(DOWN, piece(DOWN, outer), outer)
     arrived(OUT)
-    load(fulls[OUT], slot_o, 0).wait()
+    load(fulls[OUT], slot_o, first).wait()
 
     def branch_rows(index):
         return jnp.dot(mixed[tile(index, quarter), :], slot_o[...], preferred_element_type=F32)
@@ -509,7 +516,7 @@
     residual[...] += branch_rows(wires.tensor)
     to_sibling(0).wait_recv()
     residual[...] += crecv[0].astype(F32)
-    pass_on(UP)
+    hops(UP, 0, True, (2, 3))
     hops(DOWN, 0, False, (1,))
     cross.wait_recv()
     residual[...] += yrecv[...].astype(F32)
@@ -532,8 +539,25 @@
     hops(DOWN, outer, False, (1,))
     feed_cross.wait_recv()
     feed_far.start()
-    mixer_store.wait()
-    cot_loads = own_blocks(cotangent, mixer)
+    near_cols, far_cols = pl.ds(0, model // 2), pl.ds(model // 2, model // 2)
+    down_load = load(fulls[DOWN].at[:, near_cols], slot_o.at[:, near_cols], first + 1)
+    own(UP).wait()
+    up_load = load(fulls[UP].at[near_cols], slot_a.at[near_cols], first + 2)
+    for copy in cot_loads:
+        copy.wait()
+    down_load.wait()
+    gate_store.wait()
+
+    def grads_half(at, cols):
+        return lax.dot_general(
+            mixer[at, cols], slot_o[:, cols], (((1,), (1,)), ((), ())), preferred_element_type=F32
+        )
+
+    @pl.loop(0, rows)
+    def _(r):
+        at = tile(r, STEP)
+        gate_in[at, :] = grads_half(at, near_cols)
+
     hops(DOWN, outer, False, (2,))
     arrived(HIDDEN)
     load(fulls[HIDDEN], slot_b, first).wait()
@@ -541,7 +565,6 @@
     feed_far.wait_recv()
     store(wide, feed_out)
     kept_store.wait()
-    gate_store.wait()
 
     @pl.loop(0, rows)
     def _(r):
@@ -549,19 +572,16 @@
         kept[at, :] = jnp.dot(wide[at, :], slot_b[...], preferred_element_type=F32)
 
     hops(DOWN, outer, False, (3,))
-    load(fulls[DOWN], slot_o, first).wait()
-    for copy in cot_loads:
-        copy.wait()
+    load(fulls[DOWN].at[:, far_cols], slot_o.at[:, far_cols], first + 1).wait()
 
     @pl.loop(0, rows)
     def _(r):
         at = tile(r, STEP)
-        gate_in[at, :] = lax.dot_general(
-            mixer[at, :], slot_o[...], (((1,), (1,)), ((), ())), preferred_element_type=F32
-        )
+        gate_in[at, :] += grads_half(at, far_cols)
 
     arrived(UP)
-    load(fulls[UP], slot_a, first).wait()
+    load(fulls[UP].at[far_cols], slot_a.at[far_cols], first).wait()
+    up_load.wait()
     mixed_store.wait()
 
     @pl.loop(0, length // PART)
@@ -945,7 +965,8 @@
     wires.greet_all()
     n = 2 * outer
     hid_load = load(hidden_in, hid, n + 10)
-    feed_load = load(feed_in, u2, n + 2)
+    far_half, near_half = pl.ds(half, half), pl.ds(0, half)
+    feed_load = load(feed_in.at[:, far_half], u2.at[:, far_half], n + 2)
     act_load = load(activity_in, act, n + 9)
     cot_loads = own_blocks(cotangent, u0, 0)
     upg_load = load(up_in, upg, n + 11)
@@ -955,6 +976,7 @@
     gain_load = load(gains, gain_v, n + 1)
     residual_load = load(residual_in, value_q, n + 7)
     table_load = load(key_decay, keyd, n + 8)
+    near_load = load(feed_in.at[:, near_half], u2.at[:, near_half], n + 12)
     hid_load.wait()
     feed_load.wait()
     far(G_HIDDEN, u2, hid)
@@ -964,6 +986,7 @@
     upg_load.wait()
     wait_all(hidden_loads)
     wait_all(up_loads)
+    near_load.wait()
 
     def tall_terms(pairs):
         def terms(at, h):
@@ -1296,7 +1319,7 @@
         dma((3, 4)),
         dma((3 + dp_size,)),
         dma((3 + dp_size,)),
-        dma((dp_size + 12,)),
+        dma((dp_size + 13,)),
         dma((2, 2)),
         dma((N_GRADS + 1, outer)),
         dma((N_GRADS,)),

time: 640 us -> 631 us (0.986)
  Pallas kernels: 626 us -> 617 us
    pallas_call x1, Pallas kernels: 317 us -> 309 us  [forward_fast(): pl.pallas_call(kernel, out_shape=out_shape, in_specs=[ANY] * (7 + len(wei...]
where the time goes in v2:
time: 631 us; the launch traced here: 624 us
  Pallas kernels  617 us (98%)
    pallas_call x1, Pallas kernels, forward_fast(): pl.pallas_call(kernel, out_shape=out_shape, in_specs=[ANY] * (7 + len(wei...  309 us
    pallas_call x1, Pallas kernels, backward_fast(): pl.pallas_call(kernel, out_shape=out_shape, in_specs=[ANY] * len(operands...  293 us
    pallas_call x1, Pallas kernels, finish(): pl.pallas_call(kernel, grid=(steps,), out_shape=out_shape, in_specs=in_sp...  15.6 us

profile of v2, /device:TPU:0, one launch (start us, length us, event | category | flops | bytes accessed | tf_op | source)
XLA Modules:
  0.0 623.9 jit_solution(15957325285662007087)
XLA Ops:
  0.7 0.8 dynamic_update_slice.3
  1.5 0.7 pad_maximum_fusion.1
  2.1 0.8 constant_dynamic-slice_fusion.2
  2.9 0.0 copy-start
  2.9 0.6 pad_maximum_fusion.refs_24_
  3.6 0.6 broadcast_in_dim.10.refs_2_
  4.2 1.0 copy.31.refs_5_
  5.2 0.0 copy-done
  5.2 308.7 %shard_map.273 = (bf16[128,1536]{1,0:T(8,128)(2,1)}, bf16[2048,512]{1,0:T(8,128)(2,1)}, bf16[2048,512]{1,0:T(8,128)(2,1)}, bf16[2048,1024]{1,0:T(8,128)(2,1)}, b...) custom-call(bf16[1024,2048]{1,0:T(8,128)(2,1)} %refs_0_.3, ...), custom_call_target="tpu_custom_call" | custom-call | tf_op jit(solution)/shard_map/pallas_call | solution.py:703
  314.0 292.7 %shard_map.274 = (bf16[1024,2048]{1,0:T(8,128)(2,1)}, bf16[1024,2048]{1,0:T(8,128)(2,1)}, f32[7,256,1024]{2,1,0:T(8,128)}, bf16[8,3,256,1024]{3,2,1,0:T(8,128)(2...) custom-call(bf16[1024,2048]{1,0:T(8,128)(2,1)} %refs_0_.3, ...), custom_call_target="tpu_custom_call" | custom-call | tf_op jit(solution)/shard_map/pallas_call | solution.py:1332
  606.6 0.0 copy-start.1
  606.7 15.6 %shard_map.275 = (f32[256,512]{1,0:T(8,128)}, f32[256,512]{1,0:T(8,128)}, f32[256,1024]{1,0:T(8,128)}, f32[256,1024]{1,0:T(8,128)}, f32[1024,256]{1,0:T(8,128)},...) custom-call(f32[7,256,1024]{2,1,0:T(8,128)} %get-tuple-element.71.re, ...), custom_call_target="tpu_custom_call" | custom-call | tf_op jit(solution)/shard_map/pallas_call | solution.py:1399
  622.3 0.0 copy-done.1
  622.3 0.6 fusion
  622.9 0.6 constant_dynamic-slice_fusion
  (4 shorter events, 0.0 us)
Async XLA Ops:
  2.9 2.3 copy-start
  606.6 15.6 %copy-start.1 = (f32[8,256]{1,0:T(8,128)S(1)}, f32[8,256]{1,0:T(8,128)}, u32[]{:S(2)}) copy-start(f32[8,256]{1,0:T(8,128)} %get-tuple-element.78) | copy-start | bytes 24580

commit v3 on v2

--- a/solution.py
+++ b/solution.py
@@ -250,14 +250,14 @@
 def forward_kernel(outer, heads, dims, *refs):
     length, model, block = dims
     quarter = length // 4
-    tokens, cotangent, gains, cosine, sine, row_decay, key_decay = refs[:7]
-    items = (gains,) + refs[7:15]
-    fulls = refs[15:24]
+    tokens, cotangent, gains, cosine, sine, decays = refs[:6]
+    items = (gains,) + refs[6:14]
+    fulls = refs[14:23]
     (mixer_out, query_out, key_out, value_out, retained_out, gate_out, mixed_out, residual_out,
-     feed_out, hidden_out, up_out, activity_out) = refs[24:36]
+     feed_out, hidden_out, up_out, activity_out) = refs[23:35]
     (slot_a, slot_b, slot_o, wide, mixer, rq, rk, values, kept, gate_in, mixed, residual, csend, crecv, ysend,
-     yrecv, cos_v, sin_v, rowd, keyd, gain_v, gain_m, gain_f, gain_g,
-     loc, zs, zr, xs, xr, ts, tr, ls, os_) = refs[36:]
+     yrecv, cos_v, sin_v, keyd, gain_v, gain_m, gain_f, gain_g,
+     loc, zs, zr, xs, xr, ts, tr, ls, os_) = refs[35:]
     wires = Wires(outer)
     rows = length // STEP
     units = slot_a.shape[1]
@@ -387,8 +387,7 @@
     loads = own_blocks(tokens, wide)
     loads.append(load(cosine, cos_v, first))
     loads.append(load(sine, sin_v, first + 1))
-    loads.append(load(row_decay, rowd, first + 2))
-    loads.append(load(key_decay, keyd, first + 3))
+    loads.append(load(decays.at[wires.tensor], keyd, first + 2))
     own(GAINS).wait()
     for place in range(1, 2 * outer):
         gain_copy(place).wait_recv()
@@ -460,7 +459,7 @@
             q = rq[at, h * DK : (h + 1) * DK]
             k = rk[:upto, h * DK : (h + 1) * DK]
             raw = lax.dot_general(q, k, (((1,), (1,)), ((), ())), preferred_element_type=F32)
-            fade = rowd[at, h : h + 1] * keyd[h : h + 1, :upto]
+            fade = keyd[heads + h : heads + h + 1, at].reshape(STEP, 1) * keyd[h : h + 1, :upto]
             place = lax.broadcasted_iota(jnp.int32, (STEP, upto), 0) + r * STEP
             under = place >= lax.broadcasted_iota(jnp.int32, (STEP, upto), 1)
             scores = raw * jnp.where(under, fade, 0.0)
@@ -584,21 +583,24 @@
     up_load.wait()
     mixed_store.wait()
 
-    @pl.loop(0, length // PART)
-    def _(r):
-        at = tile(r, PART)
-        u = jnp.dot(wide[at, :], slot_a[...], preferred_element_type=F32)
-        h, grads = kept[at, :], gate_in[at, :]
-        t = jnp.tanh(SQRT_2_PI * (h + CUBIC * h * h * h))
-        gelu = 0.5 * h * (1.0 + t)
-        slope = 0.5 * (1.0 + t) + 0.5 * h * (1.0 - t * t) * (SQRT_2_PI * (1.0 + 3.0 * CUBIC * h * h))
-        mixed[at, :] = (gelu * u).astype(BF16)
-        slot_b[at, :] = (grads * u * slope).astype(BF16)
-        slot_o[at, pl.ds(0, units)] = (grads * gelu).astype(BF16)
-
-    store(mixed, activity_out)
-    store(slot_b.at[pl.ds(0, length)], hidden_out)
-    store(slot_o.at[:, pl.ds(0, units)], up_out)
+    for part in range(2):
+        @pl.loop(part * (length // PART // 2), (part + 1) * (length // PART // 2))
+        def _(r):
+            at = tile(r, PART)
+            u = jnp.dot(wide[at, :], slot_a[...], preferred_element_type=F32)
+            h, grads = kept[at, :], gate_in[at, :]
+            t = jnp.tanh(SQRT_2_PI * (h + CUBIC * h * h * h))
+            gelu = 0.5 * h * (1.0 + t)
+            slope = 0.5 * (1.0 + t) + 0.5 * h * (1.0 - t * t) * (SQRT_2_PI * (1.0 + 3.0 * CUBIC * h * h))
+            mixed[at, :] = (gelu * u).astype(BF16)
+            slot_b[at, :] = (grads * u * slope).astype(BF16)
+            slot_o[at, pl.ds(0, units)] = (grads * gelu).astype(BF16)
+
+        done = pl.ds(part * (length // 2), length // 2)
+        store(mixed.at[done], activity_out.at[done])
+        store(slot_b.at[done], hidden_out.at[done])
+        store(slot_o.at[done, pl.ds(0, units)], up_out.at[done])
+
     for copy in stores:
         if not any(copy is done for done in (kept_store, gate_store, mixer_store, mixed_store)):
             copy.wait()
@@ -615,18 +617,21 @@
     climb_sent(DOWN, outer)
 
 
-def position_tables(length, heads):
+def position_tables(length, teams, heads):
     half = DK // 2
     speeds = 10000.0 ** (-np.arange(half, dtype=np.float32) / np.float32(half))
     angles = np.arange(length, dtype=np.float32)[:, None] * speeds.astype(np.float32)[None, :]
     pair = [np.cos(angles), np.sin(angles)]
     turns = [t.reshape(length // PART, PART, half).swapaxes(0, 1).reshape(PART, -1) for t in pair]
-    rates = np.log1p(-np.exp2(-5.0 - np.arange(heads, dtype=np.float64)))[:, None]
+    rates = np.log1p(-np.exp2(-5.0 - np.arange(teams * heads, dtype=np.float64)))[:, None]
     places = np.arange(length, dtype=np.float64)[None, :]
     sums = np.expm1(rates * (places + 1)) / np.expm1(rates)
     row_decay = np.exp(rates * (places - length // 2)) / np.sqrt(sums) * DK**-0.5
     key_decay = np.exp(rates * (length // 2 - places))
-    return [jnp.asarray(np.asarray(t, np.float32)) for t in (*pair, np.stack(turns), row_decay, key_decay)]
+    fades = np.zeros((teams, 8, length))
+    fades[:, :heads] = key_decay.reshape(teams, heads, length)
+    fades[:, heads : 2 * heads] = row_decay.reshape(teams, heads, length)
+    return [jnp.asarray(np.asarray(t, np.float32)) for t in (*pair, np.stack(turns), fades)]
 
 
 def forward_fast(dp_size, tokens, cotangent, gains, tables, weights):
@@ -680,8 +685,7 @@
         pltpu.VMEM((quarter, model), BF16),
         pltpu.VMEM(tables[0].shape, F32),
         pltpu.VMEM(tables[1].shape, F32),
-        pltpu.VMEM(tables[2].shape, F32),
-        pltpu.VMEM(tables[3].shape, F32),
+        pltpu.VMEM(tables[2].shape[1:], F32),
         pltpu.VMEM(shapes[0], BF16),
         pltpu.VMEM((1, model), F32),
         pltpu.VMEM((1, model), F32),
@@ -694,7 +698,7 @@
         dma((6,)),
         dma((6,)),
         dma((2 * outer + 4,)),
-        dma((14,)),
+        dma((16,)),
     ]
 
     def kernel(*refs):
@@ -703,7 +707,7 @@
     results = pl.pallas_call(
         kernel,
         out_shape=out_shape,
-        in_specs=[ANY] * (7 + len(weights)),
+        in_specs=[ANY] * (6 + len(weights)),
         out_specs=[ANY] * len(out_shape),
         scratch_shapes=scratch,
         compiler_params=pltpu.CompilerParams(
@@ -975,7 +979,7 @@
     down_load = load(down_full, u1, n)
     gain_load = load(gains, gain_v, n + 1)
     residual_load = load(residual_in, value_q, n + 7)
-    table_load = load(key_decay, keyd, n + 8)
+    table_load = load(key_decay.at[wires.tensor], keyd, n + 8)
     near_load = load(feed_in.at[:, near_half], u2.at[:, near_half], n + 12)
     hid_load.wait()
     feed_load.wait()
@@ -1299,7 +1303,7 @@
         vmem((quarter, model), BF16),
         vmem((quarter, model), F32),
         vmem((quarter, model), F32),
-        vmem(tables[1].shape, F32),
+        vmem(tables[1].shape[1:], F32),
         vmem(gains.shape, BF16),
         vmem((1, model), F32),
         vmem((1, model), F32),
@@ -1446,19 +1450,16 @@
         )
 
     units = hidden_weight.shape[1]
-    even = units == 2 * width == heads_here * DV == model // 2 and heads_here * DV // block <= 6
+    even = units == 2 * width == heads_here * DV == model // 2 and heads_here * DV // block <= 6 and heads_here <= 4
     if even and block % 128 == 0 and tensor_size == 4 and dp_size == 8 and length % 1024 == 0:
         group_line = lax.dynamic_update_slice(
             jnp.zeros((heads_here, DV), BF16), group_gain, (0, data.me * group_block)
         )
         gains = jnp.concatenate([mixer_gain, feed_gain, group_line.reshape(-1)])
         gains = jnp.broadcast_to(gains[None, :], (16, gains.shape[0]))
-        cosine, sine, turns, row_decays, key_decays = position_tables(length, query_weight.shape[1] * tensor_size // DK)
-        first = lax.axis_index("tensor") * heads_here
-        row_decay = lax.dynamic_slice_in_dim(row_decays, first, heads_here, 0)
-        key_decay = lax.dynamic_slice_in_dim(key_decays, first, heads_here, 0)
-        tables = (cosine, sine, row_decay.T, key_decay)
-        back_tables = (turns, jnp.concatenate([key_decay, row_decay]))
+        cosine, sine, turns, fades = position_tables(length, tensor_size, heads_here)
+        tables = (cosine, sine, fades)
+        back_tables = (turns, fades)
         fulls, kept = forward_fast(
             dp_size,
             tokens,

time: 631 us -> 628 us (level)
  no operation moved by 1% of the time
where the time goes in v3:
time: 628 us; the launch traced here: 621 us
  Pallas kernels  616 us (98%)
    pallas_call x1, Pallas kernels, forward_fast(): pl.pallas_call(kernel, out_shape=out_shape, in_specs=[ANY] * (6 + len(wei...  308 us
    pallas_call x1, Pallas kernels, backward_fast(): pl.pallas_call(kernel, out_shape=out_shape, in_specs=[ANY] * len(operands...  293 us
    pallas_call x1, Pallas kernels, finish(): pl.pallas_call(kernel, grid=(steps,), out_shape=out_shape, in_specs=in_sp...  15.6 us

profile of v3, /device:TPU:0, one launch (start us, length us, event | category | flops | bytes accessed | tf_op | source)
XLA Modules:
  0.0 620.6 jit_solution(15798974517737205679)
XLA Ops:
  0.7 0.8 dynamic_update_slice.3
  1.5 0.7 pad_maximum_fusion
  2.1 0.6 broadcast_in_dim.10.refs_2_
  2.8 307.9 %shard_map.264 = (bf16[128,1536]{1,0:T(8,128)(2,1)}, bf16[2048,512]{1,0:T(8,128)(2,1)}, bf16[2048,512]{1,0:T(8,128)(2,1)}, bf16[2048,1024]{1,0:T(8,128)(2,1)}, b...) custom-call(bf16[1024,2048]{1,0:T(8,128)(2,1)} %refs_0_.3, ...), custom_call_target="tpu_custom_call" | custom-call | tf_op jit(solution)/shard_map/pallas_call | solution.py:707
  310.7 292.7 %shard_map.265 = (bf16[1024,2048]{1,0:T(8,128)(2,1)}, bf16[1024,2048]{1,0:T(8,128)(2,1)}, f32[7,256,1024]{2,1,0:T(8,128)}, bf16[8,3,256,1024]{3,2,1,0:T(8,128)(2...) custom-call(bf16[1024,2048]{1,0:T(8,128)(2,1)} %refs_0_.3, ...), custom_call_target="tpu_custom_call" | custom-call | tf_op jit(solution)/shard_map/pallas_call | solution.py:1336
  603.4 0.0 copy-start
  603.4 15.6 %shard_map.266 = (f32[256,512]{1,0:T(8,128)}, f32[256,512]{1,0:T(8,128)}, f32[256,1024]{1,0:T(8,128)}, f32[256,1024]{1,0:T(8,128)}, f32[1024,256]{1,0:T(8,128)},...) custom-call(f32[7,256,1024]{2,1,0:T(8,128)} %get-tuple-element.71.re, ...), custom_call_target="tpu_custom_call" | custom-call | tf_op jit(solution)/shard_map/pallas_call | solution.py:1403
  619.0 0.0 copy-done
  619.0 0.6 fusion
  619.6 0.6 constant_dynamic-slice_fusion
  (4 shorter events, 0.0 us)
Async XLA Ops:
  603.4 15.6 %copy-start = (f32[8,256]{1,0:T(8,128)S(1)}, f32[8,256]{1,0:T(8,128)}, u32[]{:S(2)}) copy-start(f32[8,256]{1,0:T(8,128)} %get-tuple-element.78) | copy-start | bytes 24580

commit v4 on v3

--- a/solution.py
+++ b/solution.py
@@ -584,7 +584,7 @@
     mixed_store.wait()
 
     for part in range(2):
-        @pl.loop(part * (length // PART // 2), (part + 1) * (length // PART // 2))
+        @pl.loop(part * (length // PART // 2), (part + 1) * (length // PART // 2), unroll=True)
         def _(r):
             at = tile(r, PART)
             u = jnp.dot(wide[at, :], slot_a[...], preferred_element_type=F32)

time: 628 us -> 627 us (level)
  no operation moved by 1% of the time
where the time goes in v4:
time: 627 us; the launch traced here: 620 us
  Pallas kernels  616 us (98%)
    pallas_call x1, Pallas kernels, forward_fast(): pl.pallas_call(kernel, out_shape=out_shape, in_specs=[ANY] * (6 + len(wei...  307 us
    pallas_call x1, Pallas kernels, backward_fast(): pl.pallas_call(kernel, out_shape=out_shape, in_specs=[ANY] * len(operands...  293 us
    pallas_call x1, Pallas kernels, finish(): pl.pallas_call(kernel, grid=(steps,), out_shape=out_shape, in_specs=in_sp...  15.6 us

profile of v4, /device:TPU:0, one launch (start us, length us, event | category | flops | bytes accessed | tf_op | source)
XLA Modules:
  0.0 620.1 jit_solution(8610254632792429045)
XLA Ops:
  0.7 0.8 dynamic_update_slice.3
  1.5 0.7 pad_maximum_fusion
  2.1 0.6 broadcast_in_dim.10.refs_2_
  2.8 307.4 %shard_map.264 = (bf16[128,1536]{1,0:T(8,128)(2,1)}, bf16[2048,512]{1,0:T(8,128)(2,1)}, bf16[2048,512]{1,0:T(8,128)(2,1)}, bf16[2048,1024]{1,0:T(8,128)(2,1)}, b...) custom-call(bf16[1024,2048]{1,0:T(8,128)(2,1)} %refs_0_.3, ...), custom_call_target="tpu_custom_call" | custom-call | tf_op jit(solution)/shard_map/pallas_call | solution.py:707
  310.2 292.7 %shard_map.265 = (bf16[1024,2048]{1,0:T(8,128)(2,1)}, bf16[1024,2048]{1,0:T(8,128)(2,1)}, f32[7,256,1024]{2,1,0:T(8,128)}, bf16[8,3,256,1024]{3,2,1,0:T(8,128)(2...) custom-call(bf16[1024,2048]{1,0:T(8,128)(2,1)} %refs_0_.3, ...), custom_call_target="tpu_custom_call" | custom-call | tf_op jit(solution)/shard_map/pallas_call | solution.py:1336
  602.9 0.0 copy-start
  602.9 15.6 %shard_map.266 = (f32[256,512]{1,0:T(8,128)}, f32[256,512]{1,0:T(8,128)}, f32[256,1024]{1,0:T(8,128)}, f32[256,1024]{1,0:T(8,128)}, f32[1024,256]{1,0:T(8,128)},...) custom-call(f32[7,256,1024]{2,1,0:T(8,128)} %get-tuple-element.71.re, ...), custom_call_target="tpu_custom_call" | custom-call | tf_op jit(solution)/shard_map/pallas_call | solution.py:1403
  618.5 0.0 copy-done
  618.5 0.6 fusion
  619.1 0.6 constant_dynamic-slice_fusion
  (4 shorter events, 0.0 us)
Async XLA Ops:
  602.9 15.6 %copy-start = (f32[8,256]{1,0:T(8,128)S(1)}, f32[8,256]{1,0:T(8,128)}, u32[]{:S(2)}) copy-start(f32[8,256]{1,0:T(8,128)} %get-tuple-element.78) | copy-start | bytes 24580
